TPU v7x, 32 devices: a whole 2x2x4 slice. The times are simulated.
32 devices in a mesh: seq: 8 (over z, x), ch: 4 (over y, core).
Axes of the slice: x: 2, y: 2, z: 4, core: 2. Of those that a mesh axis runs over, the one named last changes fastest.
Arguments:
- projected: bfloat16 [1024, 3, 4096], P('seq', None, 'ch'), may hold values from -6 to 6
- cotangent: bfloat16 [1024, 4096], P('seq', 'ch'), may hold values from -6 to 6
- short_weight: float32 [3, 7, 4096], P(None, None, 'ch'), may hold values from -2 to 2
- long_filter: float32 [8, 1024], P('ch', 'seq'), may hold values from -0.1875 to 0.1875
Outputs:
- grad_proj: bfloat16 [1024, 3, 4096], P('seq', None, 'ch')
- grad_short: float32 [3, 7, 4096], P(None, None, 'ch')
- grad_filter: float32 [8, 1024], P(None, ('seq', 'ch'))
All inputs are finite; a program needn't handle non-finite values.
Results may differ from a plain program's by a relative error of at most 0.00155.
Values may be sent and summed in bfloat16 or wider, within the bound.
A program may use at most 64 MiB of HBM per device.

v0:
```python
import math

import jax
import jax.numpy as jnp
from jax import lax
from jax.sharding import PartitionSpec as P

highest = lax.Precision.HIGHEST


def passed_along(block, axis, distance):
    devices = range(lax.axis_size(axis))
    route = [(i - distance, i) for i in devices if i - distance in devices]
    return lax.ppermute(block, axis, route)


def einsum_high(form, table, operand):
    return jnp.einsum(form, table, operand, precision=highest)


def angle_table(first, second, length):
    product = first[:, None] * second[None, :] % length
    radians = product.astype(jnp.float32) * (2.0 * math.pi / length)
    return (jnp.cos(radians), jnp.sin(radians))


def complex_dft(cosine, sine, real_part, imag_part, joined, sign):
    table = jnp.stack(
        [jnp.stack([cosine, -sign * sine], 0), jnp.stack([sign * sine, cosine], 0)], 0
    )
    stacked = jnp.stack([real_part, imag_part], 0)
    result = jnp.einsum(joined, table, stacked, precision=highest)
    return (result[0], result[1])


def rotate(real_part, imag_part, cosine, sine, sign):
    return (
        real_part * cosine - sign * imag_part * sine,
        imag_part * cosine + sign * real_part * sine,
    )


def combine(mixed_re, mixed_im, grad_re, grad_im, filt_re, filt_im):
    conv_re = filt_re * mixed_re - filt_im * mixed_im
    conv_im = filt_re * mixed_im + filt_im * mixed_re
    corr_re = filt_re * grad_re + filt_im * grad_im
    corr_im = filt_re * grad_im - filt_im * grad_re
    cross_re = mixed_re * grad_re + mixed_im * grad_im
    cross_im = mixed_re * grad_im - mixed_im * grad_re
    return (conv_re - corr_im, conv_im + corr_re, cross_re, cross_im)


def featurize(extended, weights, row_count):
    tap_count = weights.shape[1]
    accumulated = jnp.zeros((row_count,) + extended.shape[1:], jnp.float32)
    for offset in range(tap_count):
        first_row = tap_count - 1 - offset
        accumulated = accumulated + weights[:, offset, :] * extended[
            first_row : first_row + row_count
        ].astype(jnp.float32)
    return accumulated


def transpose_pair(signals, filters):
    return (
        lax.all_to_all(signals, "seq", split_axis=0, concat_axis=1, tiled=True),
        lax.all_to_all(filters, "seq", split_axis=0, concat_axis=1, tiled=True),
    )


def sequence_plan(mixed_input, gated_grad, long_filter):
    row_count, chan_count = mixed_input.shape
    group_count = long_filter.shape[0]
    seq_count = lax.axis_size("seq")
    seq_index = lax.axis_index("seq")
    per_block = row_count // seq_count
    fft_length = 2 * row_count * seq_count
    freq_index = jnp.arange(2 * seq_count, dtype=jnp.int32)
    block_index = jnp.arange(seq_count, dtype=jnp.int32)
    row_index = jnp.arange(row_count, dtype=jnp.int32)
    signals = jnp.stack([mixed_input, gated_grad], 1)[:, None]
    filters = jnp.transpose(long_filter)[:, None]
    sig_cols, filt_cols = transpose_pair(signals, filters)
    cos_one, sin_one = angle_table(freq_index, block_index, 2 * seq_count)
    sig_re = einsum_high("kb,abxc->kaxc", cos_one, sig_cols)
    sig_im = -einsum_high("kb,abxc->kaxc", sin_one, sig_cols)
    filt_re = einsum_high("kb,abg->kag", cos_one, filt_cols)
    filt_im = -einsum_high("kb,abg->kag", sin_one, filt_cols)
    positions = seq_index * per_block + jnp.arange(per_block, dtype=jnp.int32)
    cos_twist, sin_twist = angle_table(freq_index, positions, fft_length)
    sig_re, sig_im = rotate(
        sig_re, sig_im, cos_twist[:, :, None, None], sin_twist[:, :, None, None], -1.0
    )
    filt_re, filt_im = rotate(filt_re, filt_im, cos_twist[:, :, None], sin_twist[:, :, None], -1.0)
    sig_rows, filt_rows = transpose_pair(
        jnp.stack([sig_re, sig_im], 2), jnp.stack([filt_re, filt_im], 2)
    )
    cos_two, sin_two = angle_table(row_index, row_index, row_count)
    spec_re, spec_im = complex_dft(
        cos_two, sin_two, sig_rows[:, :, 0], sig_rows[:, :, 1], "pqka,qjaxc->pjkxc", -1.0
    )
    hspec_re, hspec_im = complex_dft(
        cos_two, sin_two, filt_rows[:, :, 0], filt_rows[:, :, 1], "pqka,qjag->pjkg", -1.0
    )
    leading = spec_re.shape[:2]
    group_shape = leading + (group_count, chan_count // group_count)
    wave_re, wave_im, cross_re, cross_im = combine(
        spec_re[:, :, 0].reshape(group_shape),
        spec_im[:, :, 0].reshape(group_shape),
        spec_re[:, :, 1].reshape(group_shape),
        spec_im[:, :, 1].reshape(group_shape),
        hspec_re[..., None],
        hspec_im[..., None],
    )
    wave_re = wave_re.reshape(leading + (chan_count,))
    wave_im = wave_im.reshape(leading + (chan_count,))
    cross_re = jnp.sum(cross_re, -1)
    cross_im = jnp.sum(cross_im, -1)
    back_re, back_im = complex_dft(cos_two, sin_two, wave_re, wave_im, "pqak,qjkc->pajc", 1.0)
    cback_re, cback_im = complex_dft(cos_two, sin_two, cross_re, cross_im, "pqak,qjkg->pajg", 1.0)
    pair_freq = seq_index * 2 + jnp.arange(2, dtype=jnp.int32)
    cos_back, sin_back = angle_table(row_index, pair_freq, fft_length)
    back_re, back_im = rotate(back_re, back_im, cos_back[:, :, None], sin_back[:, :, None], 1.0)
    cback_re, cback_im = rotate(cback_re, cback_im, cos_back[:, :, None], sin_back[:, :, None], 1.0)
    wave_cols, cross_cols = transpose_pair(
        jnp.stack([back_re, back_im], 2), jnp.stack([cback_re, cback_im], 2)
    )
    cos_three, sin_three = angle_table(block_index, freq_index, 2 * seq_count)
    time_re, time_im = complex_dft(
        cos_three, sin_three, wave_cols[:, :, 0], wave_cols[:, :, 1], "pqbk,qakc->pbac", 1.0
    )
    cross_time = einsum_high("bk,akg->bag", cos_three, cross_cols[:, :, 0]) - einsum_high(
        "bk,akg->bag", sin_three, cross_cols[:, :, 1]
    )
    inverse_scale = 1.0 / fft_length
    wave_out, cross_out = transpose_pair(
        jnp.stack([time_re, time_im], 2) * inverse_scale, cross_time * inverse_scale
    )
    return (wave_out[0, :, 0], wave_out[0, :, 1], jnp.transpose(cross_out[0]))


def local(projected, cotangent, short_weight, long_filter):
    tap_count = short_weight.shape[1]
    row_count = projected.shape[0]
    margin = tap_count - 1
    front_rows = passed_along(projected[row_count - margin :], "seq", 1)
    extended = jnp.concatenate([front_rows, projected], 0)
    features = featurize(extended, short_weight, row_count)
    grad_out = cotangent.astype(jnp.float32)
    mixed_input = features[:, 1] * features[:, 2]
    gated_grad = grad_out * features[:, 0]
    conv_out, corr_out, filt_grad = sequence_plan(mixed_input, gated_grad, long_filter)
    token_count = row_count * lax.axis_size("seq")
    group_width = mixed_input.shape[1] // long_filter.shape[0]
    scaled_grad = filt_grad * (1.0 / math.sqrt(token_count * group_width))
    owned_grad = lax.all_to_all(scaled_grad, "ch", split_axis=1, concat_axis=0, tiled=True)
    feat_grad = jnp.stack(
        [grad_out * conv_out, corr_out * features[:, 2], corr_out * features[:, 1]], 1
    )
    next_rows = passed_along(feat_grad[:margin].astype(jnp.bfloat16), "seq", -1).astype(jnp.float32)
    extended_grad = jnp.concatenate([feat_grad, next_rows], 0)
    grad_proj = jnp.zeros(feat_grad.shape, jnp.float32)
    for offset in range(tap_count):
        grad_proj = (
            grad_proj + short_weight[:, offset, :] * extended_grad[offset : offset + row_count]
        )
    short_terms = []
    for offset in range(tap_count):
        first_row = margin - offset
        short_terms.append(
            jnp.sum(feat_grad * extended[first_row : first_row + row_count].astype(jnp.float32), 0)
        )
    grad_short = lax.psum(jnp.stack(short_terms, 1), "seq") * (1.0 / math.sqrt(token_count))
    return (grad_proj.astype(jnp.bfloat16), grad_short, owned_grad)


def solution(mesh):
    return jax.shard_map(
        local,
        mesh=mesh,
        in_specs=(P("seq", None, "ch"), P("seq", "ch"), P(None, None, "ch"), P("ch", "seq")),
        out_specs=(P("seq", None, "ch"), P(None, None, "ch"), P(None, ("seq", "ch"))),
        check_vma=False,
    )
```

profile of v0, /device:TPU:0, one launch (start us, length us, event | category | flops | bytes accessed | tf_op | source)
XLA Modules:
  0.0 397.7 jit_solution(6109301291173310587)
XLA Ops:
  8.0 4.8 %collective-permute-start = (bf16[6,3,1024]{2,0,1:T(8,128)(2,1)S(1)}, bf16[6,3,1024]{2,0,1:T(8,128)(2,1)S(1)}, u32[]{:S(2)}, u32[]{:S(2)}) collective-permute-start(bf16[6,3,1024]{2,0,1:T(8,128)(2,1)S(1)} %slice.165), channel_id=1, source_target_pairs={{0,4},{4,8},{8,12},{12,16},{16,20},{20,24},{24,28},{1,5},{5,9},{9,... | collective-permute-start | bytes 110600 | tf_op jit(solution)/shard_map/ppermute | solution.py:14
  14.3 4.9 %all-to-all-start = ((f32[128,1,2]{2,1,0:T(1,128)}), f32[128,1,2]{2,1,0:T(1,128)S(1)}, u32[]{:S(2)}, u32[]{:S(2)}) async-start(f32[128,1,2]{2,1,0:T(1,128)} %bitcast.10), calls=%async_computation | async-start | bytes 131072 | tf_op jit(solution)/shard_map/all_to_all | solution.py:67
  20.7 4.6 %fusion.16 = f32[128,3,1024]{2,0,1:T(8,128)S(1)} fusion(bf16[128,3,1024]{2,0,1:T(8,128)(2,1)} %param.4, bf16[6,3,1024]{2,0,1:T(8,128)(2,1)S(1)} %collective-permute-done, f32[3,1024]{1,0:T(4,128)S(1)} %get-tuple-element.77, f32[3,1024]{1,0:T(4,128)S(1)} %get-tuple-element.78, f32[3,1024]{1,0:T(4,128)S(1)} %get-tuple-element.79, ...), kind=kLoop, calls=%fused_computation.54 | loop fusion | flops 14942208 | bytes 2482176 | tf_op jit(solution)/shard_map/add | solution.py:58
  28.3 6.0 %all-to-all-start.2 = ((f32[128,1,2,1024]{3,2,1,0:T(2,128)}), f32[128,1,2,1024]{3,2,1,0:T(2,128)S(1)}, u32[]{:S(2)}, u32[]{:S(2)}) async-start(f32[128,1,2,1024]{3,2,1,0:T(2,128)} %copy.175), calls=%async_computation.2 | async-start | bytes 2097152 | tf_op jit(solution)/shard_map/all_to_all | solution.py:66
  36.0 23.5 %all-to-all-done.2 = f32[128,1,2,1024]{3,2,1,0:T(2,128)S(1)} async-done(((f32[128,1,2,1024]{3,2,1,0:T(2,128)}), f32[128,1,2,1024]{3,2,1,0:T(2,128)S(1)}, u32[]{:S(2)}, u32[]{:S(2)}) %all-to-all-start.2) | async-done | bytes 1048608 | tf_op jit(solution)/shard_map/all_to_all | solution.py:66
  59.5 3.5 all-to-all-start.1
  68.4 5.2 %copy.180 = f32[16,16,2,2,1024]{4,3,1,2,0:T(2,128)} copy(f32[16,16,2,2,1024]{4,0,3,1,2:T(8,128)S(1)} %pad_maximum_fusion) | data formatting | bytes 8388608 | tf_op jit(solution)/shard_map/stack | solution.py:96
  73.6 5.9 %all-to-all-start.3 = ((f32[16,16,2,2,1024]{4,3,1,2,0:T(2,128)}), f32[16,16,2,2,1024]{4,3,1,2,0:T(2,128)}, u32[]{:S(2)}, u32[]{:S(2)}) async-start(f32[16,16,2,2,1024]{4,3,1,2,0:T(2,128)} %copy.180), calls=%async_computation.3 | async-start | bytes 8388608 | tf_op jit(solution)/shard_map/all_to_all | solution.py:66
  83.1 89.3 %all-to-all-done.3 = f32[16,16,2,2,1024]{4,3,1,2,0:T(2,128)} async-done(((f32[16,16,2,2,1024]{4,3,1,2,0:T(2,128)}), f32[16,16,2,2,1024]{4,3,1,2,0:T(2,128)}, u32[]{:S(2)}, u32[]{:S(2)}) %all-to-all-start.3) | async-done | bytes 4194336 | tf_op jit(solution)/shard_map/all_to_all | solution.py:66
  172.4 3.9 copy.181
  181.1 2.9 copy.229
  184.0 5.1 %fusion.3 = f32[2,2,128,2,1024]{2,4,0,3,1:T(8,128)S(1)} fusion(f32[1,2,128,2,1024]{2,4,0,3,1:T(8,128)} %bitcast.354, f32[1,2,128,2,1024]{2,4,0,3,1:T(8,128)S(1)} %bitcast.353, f32[1,2,128,128]{3,2,1,0:T(8,128)S(1)} %get-tuple-element.51, f32[1,2,128,128]{3,2,1,0:T(8,128)S(1)} %get-tuple-element.61), kind=kOutput, calls=%fused_computation.13 | convolution fusion | flops 3222339584 | bytes 8650752 | tf_op jit(solution)/shard_map/pqka,qjaxc->pjkxc/dot_general | solution.py:32
  197.3 3.6 all-to-all-start.6
  209.6 4.0 all-to-all-start.7
  213.8 3.0 copy.188
  216.8 3.3 all-to-all-done.7
  220.1 3.6 all-to-all-start.4
  224.6 45.8 %all-to-all-done.4 = f32[128,2,2,1024]{3,1,2,0:T(2,128)S(1)} async-done(((f32[128,2,2,1024]{3,1,2,0:T(2,128)}), f32[128,2,2,1024]{3,1,2,0:T(2,128)S(1)}, u32[]{:S(2)}, u32[]{:S(2)}) %all-to-all-start.4) | async-done | bytes 2097184 | tf_op jit(solution)/shard_map/all_to_all | solution.py:66
  270.4 3.2 all-to-all-start.8
  276.2 2.7 all_to_all.127
  282.1 3.6 all-to-all-start.5
  285.8 26.6 %all-to-all-done.5 = f32[8,16,2,1024]{3,1,2,0:T(8,128)S(1)} async-done(((f32[8,16,2,1024]{3,1,2,0:T(8,128)}), f32[8,16,2,1024]{3,1,2,0:T(8,128)S(1)}, u32[]{:S(2)}, u32[]{:S(2)}) %all-to-all-start.5) | async-done | bytes 1048608 | tf_op jit(solution)/shard_map/all_to_all | solution.py:66
  318.3 3.9 collective-permute-done.1
  325.1 63.5 %all-reduce.2.cloned.1.call-done = f32[3,7,1024]{2,0,1:T(4,128)} async-done(((f32[3,7,1024]{2,0,1:T(4,128)}), f32[3,7,1024]{2,0,1:T(4,128)}) %all-reduce.2.cloned.1.call-update) | async-done | bytes 86032 | tf_op jit(solution)/shard_map/psum | solution.py:173
  (122 shorter events, 56.8 us)
Async XLA Ops:
  8.0 12.7 %collective-permute-start = (bf16[6,3,1024]{2,0,1:T(8,128)(2,1)S(1)}, bf16[6,3,1024]{2,0,1:T(8,128)(2,1)S(1)}, u32[]{:S(2)}, u32[]{:S(2)}) collective-permute-start(bf16[6,3,1024]{2,0,1:T(8,128)(2,1)S(1)} %slice.165), channel_id=1, source_target_pairs={{0,4},{4,8},{8,12},{12,16},{16,20},{20,24},{24,28},{1,5},{5,9},{9,... | collective-permute-start | bytes 110600 | tf_op jit(solution)/shard_map/ppermute | solution.py:14
  14.3 14.1 %all-to-all-start = ((f32[128,1,2]{2,1,0:T(1,128)}), f32[128,1,2]{2,1,0:T(1,128)S(1)}, u32[]{:S(2)}, u32[]{:S(2)}) async-start(f32[128,1,2]{2,1,0:T(1,128)} %bitcast.10), calls=%async_computation | async-start | bytes 131072 | tf_op jit(solution)/shard_map/all_to_all | solution.py:67
  20.7 4.7 %copy-start.7 = (f32[3,1,1024]{2,0,1:T(4,128)}, f32[3,1,1024]{2,0,1:T(4,128)S(1)}, u32[]{:S(2)}) copy-start(f32[3,1,1024]{2,0,1:T(4,128)S(1)} %copy.260) | copy-start | bytes 36868
  20.7 4.7 %copy-start.4 = (bf16[128,1024]{1,0:T(8,128)(2,1)S(1)}, bf16[128,1024]{1,0:T(8,128)(2,1)}, u32[]{:S(2)}) copy-start(bf16[128,1024]{1,0:T(8,128)(2,1)} %param.5) | copy-start | bytes 786436
  25.3 1.2 copy-start.1
  28.3 31.1 %all-to-all-start.2 = ((f32[128,1,2,1024]{3,2,1,0:T(2,128)}), f32[128,1,2,1024]{3,2,1,0:T(2,128)S(1)}, u32[]{:S(2)}, u32[]{:S(2)}) async-start(f32[128,1,2,1024]{3,2,1,0:T(2,128)} %copy.175), calls=%async_computation.2 | async-start | bytes 2097152 | tf_op jit(solution)/shard_map/all_to_all | solution.py:66
  59.5 14.1 %all-to-all-start.1 = ((f32[8,1,128]{2,1,0:T(1,128)}), f32[8,1,128]{2,1,0:T(1,128)S(1)}, u32[]{:S(2)}, u32[]{:S(2)}) async-start(f32[8,1,128]{2,1,0:T(1,128)} %reshape.634), calls=%async_computation.1 | async-start | bytes 8192 | tf_op jit(solution)/shard_map/all_to_all | solution.py:67
  73.6 98.8 %all-to-all-start.3 = ((f32[16,16,2,2,1024]{4,3,1,2,0:T(2,128)}), f32[16,16,2,2,1024]{4,3,1,2,0:T(2,128)}, u32[]{:S(2)}, u32[]{:S(2)}) async-start(f32[16,16,2,2,1024]{4,3,1,2,0:T(2,128)} %copy.180), calls=%async_computation.3 | async-start | bytes 8388608 | tf_op jit(solution)/shard_map/all_to_all | solution.py:66
  189.3 1.3 copy-start
  197.3 10.0 %all-to-all-start.6 = ((f32[8,1,128]{2,1,0:T(1,128)}), f32[8,1,128]{2,1,0:T(1,128)S(1)}, u32[]{:S(2)}, u32[]{:S(2)}) async-start(f32[8,1,128]{2,1,0:T(1,128)} %reshape.636), calls=%async_computation.6 | async-start | bytes 8192 | tf_op jit(solution)/shard_map/all_to_all | solution.py:67
  202.9 2.0 copy-start.9
  202.9 2.0 copy-start.10
  209.6 10.5 %all-to-all-start.7 = ((f32[8,16,2]{1,2,0:T(2,128)}), f32[8,16,2]{1,2,0:T(2,128)S(1)}, u32[]{:S(2)}, u32[]{:S(2)}) async-start(f32[8,16,2]{1,2,0:T(2,128)} %copy.199), calls=%async_computation.7 | async-start | bytes 16384 | tf_op jit(solution)/shard_map/all_to_all | solution.py:67
  220.1 50.3 %all-to-all-start.4 = ((f32[128,2,2,1024]{3,1,2,0:T(2,128)}), f32[128,2,2,1024]{3,1,2,0:T(2,128)S(1)}, u32[]{:S(2)}, u32[]{:S(2)}) async-start(f32[128,2,2,1024]{3,1,2,0:T(2,128)} %copy.188), calls=%async_computation.4 | async-start | bytes 4194304 | tf_op jit(solution)/shard_map/all_to_all | solution.py:66
  270.4 11.8 %all-to-all-start.8 = ((f32[2,4,32]{2,0,1:T(2,128)}), f32[2,4,32]{2,0,1:T(2,128)S(1)}, u32[]{:S(2)}, u32[]{:S(2)}) async-start(f32[2,4,32]{2,0,1:T(2,128)} %copy.201), calls=%async_computation.8 | async-start | bytes 8192 | tf_op jit(solution)/shard_map/all_to_all | solution.py:156
  282.1 30.2 %all-to-all-start.5 = ((f32[8,16,2,1024]{3,1,2,0:T(8,128)}), f32[8,16,2,1024]{3,1,2,0:T(8,128)S(1)}, u32[]{:S(2)}, u32[]{:S(2)}) async-start(f32[8,16,2,1024]{3,1,2,0:T(8,128)} %copy.191), calls=%async_computation.5 | async-start | bytes 2097152 | tf_op jit(solution)/shard_map/all_to_all | solution.py:66
  285.7 26.7 %copy-start.2 = (f32[128,3,1024]{2,0,1:T(8,128)S(1)}, f32[128,3,1024]{2,0,1:T(8,128)}, u32[]{:S(2)}) copy-start(f32[128,3,1024]{2,0,1:T(8,128)} %copy-done.1) | copy-start | bytes 4718596
  285.7 102.9 %all-reduce.2.cloned.1.call-start = ((), (), s32[]{:S(2)}) async-start(), calls=%async_computation.9 | async-start | bytes 229376 | tf_op jit(solution)/shard_map/psum | solution.py:173
  312.4 1.0 copy-start.5
  313.4 1.1 copy-start.3
  316.2 6.0 %collective-permute-start.1 = (bf16[6,3,1024]{2,0,1:T(8,128)(2,1)S(1)}, bf16[6,3,1024]{2,0,1:T(8,128)(2,1)S(1)}, u32[]{:S(2)}, u32[]{:S(2)}) collective-permute-start(bf16[6,3,1024]{2,0,1:T(8,128)(2,1)S(1)} %slice.407), channel_id=1, source_target_pairs={{4,0},{8,4},{12,8},{16,12},{20,16},{24,20},{28,24},{5,1},{9,5},{13... | collective-permute-start | bytes 110600 | tf_op jit(solution)/shard_map/ppermute | solution.py:14
  317.6 0.7 copy-start.6
  322.2 0.7 copy-start.8
Sparse Core Ops, SparseCore 0:
  318.4 70.1 all-reduce.1
where the time goes:
time: 399 us; the launch traced here: 398 us
  waiting for transfers between devices  258 us (65%)
  local copies, waits for them, and re-layouts  45 us (11%)
  starting transfers between devices  44.4 us (11%)
  other arithmetic  20.5 us (5%)
  matrix products  15.2 us (4%)
  between operations  14.7 us (4%)
    all_to_all x4, waiting for transfers between devices, transpose_pair(): lax.all_to_all(signals, 'seq', split_axis=0, concat_axis=1, tiled=True)  185 us
    psum x1, waiting for transfers between devices, local(): lax.psum(jnp.stack(short_terms, 1), 'seq') * (1.0 / math.sqrt(token_count))  63.5 us
    all_to_all x4, starting transfers between devices, transpose_pair(): lax.all_to_all(signals, 'seq', split_axis=0, concat_axis=1, tiled=True)  19 us
    all_to_all x4, starting transfers between devices, transpose_pair(): lax.all_to_all(filters, 'seq', split_axis=0, concat_axis=1, tiled=True)  16 us
    unnamed x42, local copies, waits for them, and re-layouts  14.9 us
    all_to_all x5, local copies, waits for them, and re-layouts, transpose_pair(): lax.all_to_all(signals, 'seq', split_axis=0, concat_axis=1, tiled=True)  9.88 us
    dot_general x5, matrix products, complex_dft(): result = jnp.einsum(joined, table, stacked, precision=highest)  9.44 us
  transfers between devices with their start and end apart: 12, of which 8 were waited for; matrix products, arithmetic and copies ran while one was open for 10% of the time, Pallas kernels for 0%

commit v1 on v0

--- a/solution.py
+++ b/solution.py
@@ -1,11 +1,18 @@
+import functools
 import math
 
 import jax
 import jax.numpy as jnp
 from jax import lax
+from jax.experimental import pallas as pl
+from jax.experimental.pallas import tpu as pltpu
 from jax.sharding import PartitionSpec as P
 
 highest = lax.Precision.HIGHEST
+MESH = pl.DeviceIdType.MESH
+LANES = 128
+WIDE = 256
+ROWS = 64
 
 
 def passed_along(block, axis, distance):
@@ -139,7 +146,369 @@
     return (wave_out[0, :, 0], wave_out[0, :, 1], jnp.transpose(cross_out[0]))
 
 
-def local(projected, cotangent, short_weight, long_filter):
+def split_halves(value):
+    top = value.astype(jnp.bfloat16)
+    rest = (value - top.astype(jnp.float32)).astype(jnp.bfloat16)
+    return top, rest
+
+
+def dot32(left, right):
+    return jnp.dot(left, right, preferred_element_type=jnp.float32)
+
+
+def dot32_t(left, right):
+    return lax.dot_general(
+        left, right, (((1,), (1,)), ((), ())), preferred_element_type=jnp.float32
+    )
+
+
+def tile(index):
+    return pl.ds(pl.multiple_of(index * LANES, LANES), LANES)
+
+
+def send_to(src, dst, send_sem, recv_sem, peer):
+    return pltpu.make_async_remote_copy(
+        src_ref=src,
+        dst_ref=dst,
+        send_sem=send_sem,
+        recv_sem=recv_sem,
+        device_id=peer,
+        device_id_type=MESH,
+    )
+
+
+def build_filters(taps, ns, low_hi, low_lo, up_hi, up_lo):
+    row = lax.broadcasted_iota(jnp.int32, (LANES, LANES), 0)
+    col = lax.broadcasted_iota(jnp.int32, (LANES, LANES), 1)
+    flip = (row + col == LANES - 1).astype(jnp.float32)
+    zero = jnp.zeros((LANES, LANES), jnp.float32)
+    zero16 = zero.astype(jnp.bfloat16)
+    flipped = jnp.dot(
+        taps[...].reshape(ns * 8, LANES), flip, precision=highest,
+        preferred_element_type=jnp.float32,
+    )
+    last_up, last_low = zero, zero
+    top = ns - WIDE // LANES
+    low_hi[:, (ns - 1) * LANES :] = jnp.concatenate([zero16, zero16], 0)
+    low_lo[:, (ns - 1) * LANES :] = jnp.concatenate([zero16, zero16], 0)
+    up_hi[LANES:, :LANES] = zero16
+    up_lo[LANES:, :LANES] = zero16
+    for d in range(ns):
+        forward = jnp.concatenate([taps[d]] * (LANES // 8), 0)
+        back = jnp.concatenate([flipped[d * 8 : d * 8 + 8]] * (LANES // 8), 0)
+        forward = pltpu.roll(forward, 0, 1, stride=1, stride_axis=0)
+        back = pltpu.roll(back, 1, 1, stride=1, stride_axis=0)
+        up = split_halves(jnp.where(col >= row, forward, last_up))
+        low = split_halves(jnp.where(row >= col, back, last_low))
+        last_up, last_low = forward, back
+        for u in range(WIDE // LANES):
+            v = d + u
+            if v < ns:
+                up_hi[u * LANES : (u + 1) * LANES, v * LANES : (v + 1) * LANES] = up[0]
+                up_lo[u * LANES : (u + 1) * LANES, v * LANES : (v + 1) * LANES] = up[1]
+            v = top + u - d
+            if 0 <= v < ns:
+                low_hi[u * LANES : (u + 1) * LANES, v * LANES : (v + 1) * LANES] = low[0]
+                low_lo[u * LANES : (u + 1) * LANES, v * LANES : (v + 1) * LANES] = low[1]
+
+
+def diagonal_sums(gram, ns):
+    row = lax.broadcasted_iota(jnp.int32, (LANES, LANES), 0)
+    col = lax.broadcasted_iota(jnp.int32, (LANES, LANES), 1)
+    turned = []
+    for d in range(ns):
+        block = gram[LANES:, d * LANES : (d + 1) * LANES]
+        if d + 1 < ns:
+            block = block + gram[:LANES, (d + 1) * LANES : (d + 2) * LANES]
+        turned.append(pltpu.roll(block, 1, 1, stride=1, stride_axis=0))
+    turned.append(jnp.zeros((LANES, LANES), jnp.float32))
+    return [
+        jnp.sum(jnp.where(col <= row, turned[d], turned[d + 1]), 0, keepdims=True)
+        for d in range(ns)
+    ]
+
+
+def resident_kernel(
+    ns, nc, kt, groups,
+    proj, cot, weight, filt,
+    gp_out, gs_out, gf_out,
+    pin, cin, wide, feat, mixed, gated, fgrad, gp_send,
+    tap_send, taps, low_hi, low_lo, up_hi, up_lo, gram,
+    fa_send, fa_recv, fb_send, fb_recv, gs_acc, gs_send, gs_recv,
+    in_send, in_recv, gp_ssem, gp_rsem, gs_ssem, gs_rsem,
+    fa_ssem, fa_rsem, fb_ssem, fb_rsem,
+):
+    me = lax.axis_index("seq")
+    mych = lax.axis_index("ch")
+    total = ns * LANES
+    tiles_per_group = ns // groups
+    seq_peers = [(lax.rem(me + i, ns), mych) for i in range(1, ns)]
+    ch_peers = [(me, lax.rem(mych + i, nc)) for i in range(1, nc)]
+
+    barrier = pltpu.get_barrier_semaphore()
+    for peer in seq_peers + ch_peers:
+        pl.semaphore_signal(barrier, inc=1, device_id=peer, device_id_type=MESH)
+    for g in range(groups):
+        tap_send[g] = jnp.broadcast_to(filt[g : g + 1, :], (8, LANES))
+    pl.semaphore_wait(barrier, ns + nc - 2)
+
+    sends = []
+    for peer in seq_peers:
+        q = peer[0]
+        copy = send_to(
+            tap_send.at[q // tiles_per_group], taps.at[me],
+            in_send.at[0, q], in_recv.at[0, me], peer,
+        )
+        copy.start()
+        sends.append(copy)
+    for peer in seq_peers:
+        q = peer[0]
+        for copy in (
+            send_to(
+                proj.at[:, :, tile(q)], pin.at[:, tile(me), :],
+                in_send.at[1, q], in_recv.at[1, me], peer,
+            ),
+            send_to(
+                cot.at[:, tile(q)], cin.at[tile(me), :],
+                in_send.at[2, q], in_recv.at[2, me], peer,
+            ),
+        ):
+            copy.start()
+            sends.append(copy)
+
+    taps[me] = tap_send[me // tiles_per_group]
+    pin[:, tile(me), :] = proj[:, :, tile(me)]
+    cin[tile(me), :] = cot[:, tile(me)]
+    for j in range(3):
+        wide[j, 0:8, :] = jnp.zeros((8, LANES), jnp.float32)
+        fgrad[j, total : total + 8, :] = jnp.zeros((8, LANES), jnp.float32)
+        for k in range(kt):
+            gs_acc[j, k] = jnp.zeros((8, LANES), jnp.float32)
+    gram[...] = jnp.zeros(gram.shape, jnp.float32)
+    for peer in seq_peers:
+        q = peer[0]
+        send_to(
+            tap_send.at[0], taps.at[q], in_send.at[0, q], in_recv.at[0, q], peer
+        ).wait_recv()
+    build_filters(taps, ns, low_hi, low_lo, up_hi, up_lo)
+
+    def featurize_block(b, carry):
+        @pl.when(b != me)
+        def _():
+            send_to(
+                proj.at[:, :, tile(b)], pin.at[:, tile(b), :],
+                in_send.at[1, b], in_recv.at[1, b], (b, mych),
+            ).wait_recv()
+            send_to(
+                cot.at[:, tile(b)], cin.at[tile(b), :],
+                in_send.at[2, b], in_recv.at[2, b], (b, mych),
+            ).wait_recv()
+
+        base = pl.multiple_of(b * LANES, LANES)
+        for j in range(3):
+            wide[j, pl.ds(base + 8, LANES), :] = pin[j, pl.ds(base, LANES), :].astype(jnp.float32)
+        for part in range(LANES // ROWS):
+            first = base + part * ROWS
+            feats = []
+            for j in range(3):
+                acc = jnp.zeros((ROWS, LANES), jnp.float32)
+                for k in range(kt):
+                    acc = acc + weight[j, k : k + 1, tile(me)] * wide[
+                        j, pl.ds(first + 8 - k, ROWS), :
+                    ]
+                feats.append(acc)
+            rows = pl.ds(first, ROWS)
+            feat[0, rows, :] = feats[1]
+            feat[1, rows, :] = feats[2]
+            top, rest = split_halves(feats[1] * feats[2])
+            mixed[rows, 0:LANES] = top
+            mixed[rows, LANES:WIDE] = rest
+            top, rest = split_halves(cin[rows, :].astype(jnp.float32) * feats[0])
+            gated[rows, 0:LANES] = top
+            gated[rows, LANES:WIDE] = rest
+        return carry
+
+    lax.fori_loop(0, ns, featurize_block, 0)
+
+    steps = total // WIDE
+    for b in range(steps):
+        rows = slice(b * WIDE, (b + 1) * WIDE)
+        upto = (b + 1) * WIDE
+        start = total - upto
+        both = dot32(low_hi[:, start:], mixed[:upto, :])
+        conv = both[:, :LANES] + both[:, LANES:]
+        conv = conv + dot32(low_lo[:, start:], mixed[:upto, :LANES])
+        fgrad[0, rows, :] = cin[rows, :].astype(jnp.float32) * conv
+        span = total - b * WIDE
+        both = dot32(up_hi[:, :span], gated[b * WIDE :, :])
+        corr = both[:, :LANES] + both[:, LANES:]
+        corr = corr + dot32(up_lo[:, :span], gated[b * WIDE :, :LANES])
+        fgrad[1, rows, :] = corr * feat[1, rows, :]
+        fgrad[2, rows, :] = corr * feat[0, rows, :]
+
+    def finish_block(i, carry):
+        b = lax.rem(me + 1 + i, ns)
+        base = pl.multiple_of(b * LANES, LANES)
+        for part in range(LANES // ROWS):
+            first = base + part * ROWS
+            for j in range(3):
+                acc = jnp.zeros((ROWS, LANES), jnp.float32)
+                source = wide[j, pl.ds(first + 8, ROWS), :]
+                for k in range(kt):
+                    shifted = fgrad[j, pl.ds(first + k, ROWS), :]
+                    acc = acc + weight[j, k : k + 1, tile(me)] * shifted
+                    terms = (shifted * source).reshape(ROWS // 8, 8, LANES)
+                    gs_acc[j, k] += jnp.sum(terms, 0)
+                gp_send[j, pl.ds(first, ROWS), :] = acc.astype(jnp.bfloat16)
+
+        @pl.when(b != me)
+        def _():
+            send_to(
+                gp_send.at[:, tile(b), :], gp_out.at[:, :, tile(me)],
+                gp_ssem.at[b], gp_rsem.at[me], (b, mych),
+            ).start()
+
+        return carry
+
+    lax.fori_loop(0, ns, finish_block, 0)
+    gp_out[:, :, tile(me)] = gp_send[:, tile(me), :]
+
+    short_scale = 1.0 / math.sqrt(total)
+    for j in range(3):
+        lines = [jnp.sum(gs_acc[j, k], 0, keepdims=True) for k in range(kt)]
+        lines += [jnp.zeros((1, LANES), jnp.float32)] * (8 - kt)
+        gs_send[j] = jnp.concatenate(lines, 0) * short_scale
+    for peer in seq_peers:
+        q = peer[0]
+        copy = send_to(gs_send, gs_recv.at[me], gs_ssem.at[q], gs_rsem.at[me], peer)
+        copy.start()
+        sends.append(copy)
+    gs_recv[me] = gs_send[...]
+
+    flip = (
+        lax.broadcasted_iota(jnp.int32, (WIDE, WIDE), 0)
+        + lax.broadcasted_iota(jnp.int32, (WIDE, WIDE), 1)
+        == WIDE - 1
+    ).astype(jnp.float32).astype(jnp.bfloat16)
+    for b in range(steps):
+        left = dot32(flip, mixed[b * WIDE : (b + 1) * WIDE, :]).astype(jnp.bfloat16)
+        for d in range(steps - b):
+            right = gated[(b + d) * WIDE : (b + d + 1) * WIDE, :]
+            top = right[:, :LANES]
+            cols = slice(d * WIDE, (d + 1) * WIDE)
+            gram[:, cols] += dot32_t(left, jnp.concatenate([top, top], 1)) + dot32_t(
+                left[:, :LANES], right[:, LANES:]
+            )
+    filter_scale = 1.0 / math.sqrt(total * tiles_per_group * LANES)
+    for d, line in enumerate(diagonal_sums(gram, ns)):
+        fa_send[d] = jnp.broadcast_to(line * filter_scale, (8, LANES))
+    for peer in seq_peers:
+        q = peer[0]
+        copy = send_to(fa_send.at[q], fa_recv.at[me], fa_ssem.at[q], fa_rsem.at[me], peer)
+        copy.start()
+        sends.append(copy)
+    fa_recv[me] = fa_send[me]
+    for peer in seq_peers:
+        q = peer[0]
+        send_to(fa_send.at[q], fa_recv.at[q], fa_ssem.at[q], fa_rsem.at[q], peer).wait_recv()
+    for g in range(groups):
+        summed = fa_recv[g * tiles_per_group]
+        for q in range(g * tiles_per_group + 1, (g + 1) * tiles_per_group):
+            summed = summed + fa_recv[q]
+        fb_send[g] = summed
+    for peer in ch_peers:
+        c = peer[1]
+        copy = send_to(fb_send, fb_recv.at[mych], fb_ssem.at[c], fb_rsem.at[mych], peer)
+        copy.start()
+        sends.append(copy)
+    fb_recv[mych] = fb_send[...]
+    for peer in ch_peers:
+        c = peer[1]
+        send_to(fb_send, fb_recv.at[c], fb_ssem.at[c], fb_rsem.at[c], peer).wait_recv()
+    width = LANES // nc
+    for c in range(nc):
+        for g in range(groups):
+            line = fb_recv[c, g]
+            mine = line[:, 0:width]
+            for other in range(1, nc):
+                piece = line[:, other * width : (other + 1) * width]
+                mine = jnp.where(mych == other, piece, mine)
+            at = c * groups + g
+            gf_out[at : at + 1, :] = mine[0:1, :]
+
+    for peer in seq_peers:
+        q = peer[0]
+        send_to(gs_send, gs_recv.at[q], gs_ssem.at[q], gs_rsem.at[q], peer).wait_recv()
+    for q in range(ns):
+        for j in range(3):
+            gs_out[j, :, q * LANES : (q + 1) * LANES] = gs_recv[q, j, 0:kt, :]
+    for peer in seq_peers:
+        q = peer[0]
+        copy = send_to(
+            gp_send.at[:, tile(q), :], gp_out.at[:, :, tile(q)],
+            gp_ssem.at[q], gp_rsem.at[q], peer,
+        )
+        copy.wait_send()
+        copy.wait_recv()
+    for copy in sends:
+        copy.wait_send()
+
+
+def resident(projected, cotangent, short_weight, long_filter):
+    row_count, streams, chan_count = projected.shape
+    kt = short_weight.shape[1]
+    groups = long_filter.shape[0]
+    ns, nc = lax.axis_size("seq"), lax.axis_size("ch")
+    total = row_count * ns
+    f32, bf16 = jnp.float32, jnp.bfloat16
+    dma = pltpu.SemaphoreType.DMA
+    vmem = pl.BlockSpec(memory_space=pltpu.VMEM)
+    grad_proj, grad_short, grad_filter = pl.pallas_call(
+        functools.partial(resident_kernel, ns, nc, kt, groups),
+        out_shape=(
+            jax.ShapeDtypeStruct((streams, row_count, chan_count), bf16),
+            jax.ShapeDtypeStruct((streams, kt, chan_count), f32),
+            jax.ShapeDtypeStruct((groups * nc, row_count // nc), f32),
+        ),
+        in_specs=[vmem] * 4,
+        out_specs=(vmem, vmem, vmem),
+        scratch_shapes=[
+            pltpu.VMEM((3, total, LANES), bf16),
+            pltpu.VMEM((total, LANES), bf16),
+            pltpu.VMEM((3, total + 8, LANES), f32),
+            pltpu.VMEM((2, total, LANES), f32),
+            pltpu.VMEM((total, WIDE), bf16),
+            pltpu.VMEM((total, WIDE), bf16),
+            pltpu.VMEM((3, total + 8, LANES), f32),
+            pltpu.VMEM((3, total, LANES), bf16),
+            pltpu.VMEM((groups, 8, LANES), f32),
+            pltpu.VMEM((ns, 8, LANES), f32),
+            pltpu.VMEM((WIDE, total), bf16),
+            pltpu.VMEM((WIDE, total), bf16),
+            pltpu.VMEM((WIDE, total), bf16),
+            pltpu.VMEM((WIDE, total), bf16),
+            pltpu.VMEM((WIDE, total), f32),
+            pltpu.VMEM((ns, 8, LANES), f32),
+            pltpu.VMEM((ns, 8, LANES), f32),
+            pltpu.VMEM((groups, 8, LANES), f32),
+            pltpu.VMEM((nc, groups, 8, LANES), f32),
+            pltpu.VMEM((3, 8, 8, LANES), f32),
+            pltpu.VMEM((3, 8, LANES), f32),
+            pltpu.VMEM((ns, 3, 8, LANES), f32),
+            dma((3, ns)), dma((3, ns)),
+            dma((ns,)), dma((ns,)),
+            dma((ns,)), dma((ns,)),
+            dma((ns,)), dma((ns,)),
+            dma((nc,)), dma((nc,)),
+        ],
+        compiler_params=pltpu.CompilerParams(
+            collective_id=0, has_side_effects=True, vmem_limit_bytes=40 * 1024 * 1024
+        ),
+    )(jnp.transpose(projected, (1, 0, 2)), cotangent, short_weight, long_filter)
+    return jnp.transpose(grad_proj, (1, 0, 2)), grad_short, grad_filter
+
+
+def spread(projected, cotangent, short_weight, long_filter):
     tap_count = short_weight.shape[1]
     row_count = projected.shape[0]
     margin = tap_count - 1
@@ -174,6 +543,21 @@
     return (grad_proj.astype(jnp.bfloat16), grad_short, owned_grad)
 
 
+def local(projected, cotangent, short_weight, long_filter):
+    row_count, _, chan_count = projected.shape
+    seq_count = lax.axis_size("seq")
+    group_width = chan_count // long_filter.shape[0]
+    fits = (
+        row_count == LANES
+        and chan_count == LANES * seq_count
+        and group_width % LANES == 0
+        and row_count * seq_count % WIDE == 0
+        and short_weight.shape[1] <= 8
+    )
+    plan = resident if fits else spread
+    return plan(projected, cotangent, short_weight, long_filter)
+
+
 def solution(mesh):
     return jax.shard_map(
         local,

time: 399 us -> 62.5 us (0.16)
  waiting for transfers between devices: 258 us -> 0 us
  Pallas kernels: 0 us -> 55.2 us
  starting transfers between devices: 44.4 us -> 0 us
  local copies, waits for them, and re-layouts: 45 us -> 5.76 us
  other arithmetic: 20.5 us -> 0 us
  matrix products: 15.2 us -> 0 us
  between operations: 14.7 us -> 0.65 us
    all_to_all x9 -> x0, waiting for transfers between devices: 191 us -> none  [the longest x4 185 us: transpose_pair(): lax.all_to_all(signals, 'seq', split_axis=0, concat_axis=1, tiled=True)]
    psum x1 -> x0, waiting for transfers between devices: 63.5 us -> none  [local(): lax.psum(jnp.stack(short_terms, 1), 'seq') * (1.0 / math.sqrt(token_count))]
    pallas_call x0 -> x1, Pallas kernels: none -> 55.2 us  [resident(): pl.pallas_call(functools.partial(resident_kernel, ns, nc, kt, groups), ou...]
    all_to_all x9 -> x0, starting transfers between devices: 38.2 us -> none  [the longest x4 19 us: transpose_pair(): lax.all_to_all(signals, 'seq', split_axis=0, concat_axis=1, tiled=True)]
    dot_general x11 -> x0, matrix products: 15.2 us -> none  [the longest x5 9.44 us: complex_dft(): result = jnp.einsum(joined, table, stacked, precision=highest)]
    all_to_all x12 -> x0, local copies, waits for them, and re-layouts: 11.6 us -> none  [the longest x5 9.88 us: transpose_pair(): lax.all_to_all(signals, 'seq', split_axis=0, concat_axis=1, tiled=True)]
    unnamed x42 -> x11, local copies, waits for them, and re-layouts: 14.9 us -> 5.76 us
    another operation x8 -> x0, local copies, waits for them, and re-layouts: 8.77 us -> none  [the longest x1 5.24 us: sequence_plan(): jnp.stack([sig_re, sig_im], 2)]
  transfers between devices with their start and end apart: 12 -> 0, of which waited for: 8 -> 0; matrix products, arithmetic and copies ran while one was open for 10% -> 0% of each run, Pallas kernels for 0% -> 0%
where the time goes in v1:
time: 62.5 us; the launch traced here: 61.6 us
  Pallas kernels  55.2 us (88%)
  local copies, waits for them, and re-layouts  5.76 us (9%)
  between operations  0.65 us (1%)
    pallas_call x1, Pallas kernels, resident(): pl.pallas_call(functools.partial(resident_kernel, ns, nc, kt, groups), ou...  55.2 us
    unnamed x11, local copies, waits for them, and re-layouts  5.76 us

profile of v1, /device:TPU:0, one launch (start us, length us, event | category | flops | bytes accessed | tf_op | source)
XLA Modules:
  0.0 61.6 jit_solution(11369779910894269343)
XLA Ops:
  0.6 0.0 copy-start.3
  0.6 0.7 %copy-done.3 = f32[2,128]{1,0:T(2,128)S(1)} copy-done((f32[2,128]{1,0:T(2,128)S(1)}, f32[2,128]{1,0:T(2,128)}, u32[]{:S(2)}) %copy-start.3) | copy-done | bytes 1048
  1.3 0.0 copy-start
  1.3 1.1 %copy-done = bf16[128,3,1024]{2,0,1:T(8,128)(2,1)S(1)} copy-done((bf16[128,3,1024]{2,0,1:T(8,128)(2,1)S(1)}, bf16[128,3,1024]{2,0,1:T(8,128)(2,1)}, u32[]{:S(2)}) %copy-start) | copy-done | bytes 786456
  2.4 0.0 copy-start.1
  2.4 0.9 %copy-done.1 = bf16[128,1024]{1,0:T(8,128)(2,1)S(1)} copy-done((bf16[128,1024]{1,0:T(8,128)(2,1)S(1)}, bf16[128,1024]{1,0:T(8,128)(2,1)}, u32[]{:S(2)}) %copy-start.1) | copy-done | bytes 262168
  3.4 0.0 copy-start.2
  3.4 0.9 %copy-done.2 = f32[3,7,1024]{2,1,0:T(8,128)S(1)} copy-done((f32[3,7,1024]{2,1,0:T(8,128)S(1)}, f32[3,7,1024]{2,1,0:T(8,128)}, u32[]{:S(2)}) %copy-start.2) | copy-done | bytes 86040
  4.3 55.2 %shard_map.67 = (bf16[3,128,1024]{2,1,0:T(8,128)(2,1)S(1)}, f32[3,7,1024]{2,1,0:T(8,128)S(1)}, f32[8,32]{1,0:T(8,128)S(1)}) custom-call(bf16[3,128,1024]{2,1,0:T(8,128)(2,1)S(1)} %bitcast.3, bf16[128,1024]{1,0:T(8,128)(2,1)S(1)} %copy-done.1, f32[3,7,1024]{2,1,0:T(8,128)S(1)} %copy-done.2, f32[2,128]{1,0:T(2,128)S(1)} %copy-done.3), custom_call_target="tpu_custom_call" | custom-call | tf_op jit(solution)/shard_map/pallas_call | solution.py:466
  59.5 0.9 %copy.10 = bf16[128,3,1024]{2,0,1:T(8,128)(2,1)} copy(bf16[128,3,1024]{2,0,1:T(8,128)(2,1)S(1)} %bitcast.2) | data formatting | bytes 1572864
  60.4 0.6 %copy.11 = f32[3,7,1024]{2,1,0:T(8,128)} copy(f32[3,7,1024]{2,1,0:T(8,128)S(1)} %get-tuple-element.13) | data formatting | bytes 172032
  61.0 0.6 copy.12
Async XLA Ops:
  0.6 0.7 %copy-start.3 = (f32[2,128]{1,0:T(2,128)S(1)}, f32[2,128]{1,0:T(2,128)}, u32[]{:S(2)}) copy-start(f32[2,128]{1,0:T(2,128)} %filt.1) | copy-start | bytes 3076
  1.3 1.1 %copy-start = (bf16[128,3,1024]{2,0,1:T(8,128)(2,1)S(1)}, bf16[128,3,1024]{2,0,1:T(8,128)(2,1)}, u32[]{:S(2)}) copy-start(bf16[128,3,1024]{2,0,1:T(8,128)(2,1)} %param.4) | copy-start | bytes 2359300
  2.4 0.9 %copy-start.1 = (bf16[128,1024]{1,0:T(8,128)(2,1)S(1)}, bf16[128,1024]{1,0:T(8,128)(2,1)}, u32[]{:S(2)}) copy-start(bf16[128,1024]{1,0:T(8,128)(2,1)} %cot.1) | copy-start | bytes 786436
  3.4 0.9 %copy-start.2 = (f32[3,7,1024]{2,1,0:T(8,128)S(1)}, f32[3,7,1024]{2,1,0:T(8,128)}, u32[]{:S(2)}) copy-start(f32[3,7,1024]{2,1,0:T(8,128)} %weight.1) | copy-start | bytes 258052

commit v2 on v0

--- a/solution.py
+++ b/solution.py
@@ -1,11 +1,18 @@
+import functools
 import math
 
 import jax
 import jax.numpy as jnp
 from jax import lax
+from jax.experimental import pallas as pl
+from jax.experimental.pallas import tpu as pltpu
 from jax.sharding import PartitionSpec as P
 
 highest = lax.Precision.HIGHEST
+MESH = pl.DeviceIdType.MESH
+LANES = 128
+WIDE = 256
+ROWS = 64
 
 
 def passed_along(block, axis, distance):
@@ -139,7 +146,565 @@
     return (wave_out[0, :, 0], wave_out[0, :, 1], jnp.transpose(cross_out[0]))
 
 
-def local(projected, cotangent, short_weight, long_filter):
+def split_halves(value):
+    top = value.astype(jnp.bfloat16)
+    rest = (value - top.astype(jnp.float32)).astype(jnp.bfloat16)
+    return top, rest
+
+
+def dot32(left, right):
+    return jnp.dot(left, right, preferred_element_type=jnp.float32)
+
+
+def dot32_t(left, right):
+    return lax.dot_general(
+        left, right, (((1,), (1,)), ((), ())), preferred_element_type=jnp.float32
+    )
+
+
+def tile(index, width=LANES):
+    return pl.ds(pl.multiple_of(index * width, width), width)
+
+
+def send_to(src, dst, send_sem, recv_sem, peer):
+    return pltpu.make_async_remote_copy(
+        src_ref=src,
+        dst_ref=dst,
+        send_sem=send_sem,
+        recv_sem=recv_sem,
+        device_id=peer,
+        device_id_type=MESH,
+    )
+
+
+def build_filters(taps, ns, low_hi, low_lo, up_hi, up_lo):
+    row = lax.broadcasted_iota(jnp.int32, (LANES, LANES), 0)
+    col = lax.broadcasted_iota(jnp.int32, (LANES, LANES), 1)
+    flip = (row + col == LANES - 1).astype(jnp.float32)
+    zero = jnp.zeros((LANES, LANES), jnp.float32)
+    zero16 = zero.astype(jnp.bfloat16)
+    flipped = jnp.dot(
+        taps[...].reshape(ns * 8, LANES), flip, precision=highest,
+        preferred_element_type=jnp.float32,
+    )
+    last_up, last_low = zero, zero
+    top = ns - WIDE // LANES
+    low_hi[:, (ns - 1) * LANES :] = jnp.concatenate([zero16, zero16], 0)
+    low_lo[:, (ns - 1) * LANES :] = jnp.concatenate([zero16, zero16], 0)
+    up_hi[LANES:, :LANES] = zero16
+    up_lo[LANES:, :LANES] = zero16
+    for d in range(ns):
+        forward = jnp.concatenate([taps[d]] * (LANES // 8), 0)
+        back = jnp.concatenate([flipped[d * 8 : d * 8 + 8]] * (LANES // 8), 0)
+        forward = pltpu.roll(forward, 0, 1, stride=1, stride_axis=0)
+        back = pltpu.roll(back, 1, 1, stride=1, stride_axis=0)
+        up = split_halves(jnp.where(col >= row, forward, last_up))
+        low = split_halves(jnp.where(row >= col, back, last_low))
+        last_up, last_low = forward, back
+        for u in range(WIDE // LANES):
+            v = d + u
+            if v < ns:
+                up_hi[u * LANES : (u + 1) * LANES, v * LANES : (v + 1) * LANES] = up[0]
+                up_lo[u * LANES : (u + 1) * LANES, v * LANES : (v + 1) * LANES] = up[1]
+            v = top + u - d
+            if 0 <= v < ns:
+                low_hi[u * LANES : (u + 1) * LANES, v * LANES : (v + 1) * LANES] = low[0]
+                low_lo[u * LANES : (u + 1) * LANES, v * LANES : (v + 1) * LANES] = low[1]
+
+
+def diagonal_sums(gram, ns):
+    row = lax.broadcasted_iota(jnp.int32, (LANES, LANES), 0)
+    col = lax.broadcasted_iota(jnp.int32, (LANES, LANES), 1)
+    turned = []
+    for d in range(ns):
+        block = gram[LANES:, d * LANES : (d + 1) * LANES]
+        if d + 1 < ns:
+            block = block + gram[:LANES, (d + 1) * LANES : (d + 2) * LANES]
+        turned.append(pltpu.roll(block, 1, 1, stride=1, stride_axis=0))
+    turned.append(jnp.zeros((LANES, LANES), jnp.float32))
+    return [
+        jnp.sum(jnp.where(col <= row, turned[d], turned[d + 1]), 0, keepdims=True)
+        for d in range(ns)
+    ]
+
+
+def dot_three(hi, lo, signal):
+    width = signal.shape[1] // 2
+    both = dot32(hi, signal)
+    return both[:, :width] + both[:, width:] + dot32(lo, signal[:, :width])
+
+
+def resident_kernel(
+    ns, nc, kt, groups,
+    proj, cot, weight_in, filt_in,
+    gp_out, gs_out, gf_out,
+    weight, filt, pin, cin, halo, wide, feat, mixed, gated, part, part_edge, fgrad, gp_send,
+    tap_send, taps, low_hi, low_lo, up_hi, up_lo, gram,
+    fa_send, fa_recv, fb_send, fb_recv, gs_acc, gs_send, gs_pair, gs_sum, gs_recv,
+    local_sem, in_send, in_recv, gp_ssem, gp_rsem, gs_ssem, gs_rsem,
+    fa_ssem, fa_rsem, fb_ssem, fb_rsem, pair_sem,
+):
+    me = lax.axis_index("seq")
+    mych = lax.axis_index("ch")
+    hs = ns // 2
+    total = ns * LANES
+    span = total // 2
+    half = me // hs
+    mine = lax.rem(me, hs)
+    own_base = pl.multiple_of(half * span, span)
+    group_owners = hs // groups
+    near = [half * hs + lax.rem(mine + i, hs) for i in range(1, hs)]
+    far = [(1 - half) * hs + lax.rem(mine + i, hs) for i in range(hs)]
+    everyone = near + far
+    ch_peers = [(me, lax.rem(mych + i, nc)) for i in range(1, nc)]
+    lanes_of = lambda q: tile(lax.rem(q, hs), WIDE)
+
+    own = [
+        pltpu.make_async_copy(filt_in, filt, local_sem.at[0]),
+        pltpu.make_async_copy(weight_in.at[:, :, lanes_of(me)], weight, local_sem.at[1]),
+        pltpu.make_async_copy(proj.at[:, :, lanes_of(me)], pin.at[:, tile(me), :], local_sem.at[2]),
+        pltpu.make_async_copy(cot.at[:, lanes_of(me)], cin.at[tile(me), :], local_sem.at[3]),
+    ]
+    for copy in own:
+        copy.start()
+    barrier = pltpu.get_barrier_semaphore()
+    for q in everyone:
+        pl.semaphore_signal(barrier, inc=1, device_id=(q, mych), device_id_type=MESH)
+    for peer in ch_peers:
+        pl.semaphore_signal(barrier, inc=1, device_id=peer, device_id_type=MESH)
+    own[0].wait()
+    for g in range(groups):
+        tap_send[g] = jnp.broadcast_to(filt[g : g + 1, :], (8, LANES))
+    pl.semaphore_wait(barrier, ns + nc - 2)
+
+    def tap_copy(q, src):
+        return send_to(
+            tap_send.at[lax.rem(q, hs) // group_owners], taps.at[src],
+            in_send.at[0, q], in_recv.at[0, src], (q, mych),
+        )
+
+    def halo_copy(q, src, first):
+        return send_to(
+            proj.at[:, pl.ds(first, 16), lanes_of(q)], halo,
+            in_send.at[3, q], in_recv.at[3, 0], (q, mych),
+        )
+
+    def near_copies(q, src):
+        return (
+            send_to(
+                proj.at[:, :, lanes_of(q)], pin.at[:, tile(src), :],
+                in_send.at[1, q], in_recv.at[1, src], (q, mych),
+            ),
+            send_to(
+                cot.at[:, lanes_of(q)], cin.at[tile(src), :],
+                in_send.at[2, q], in_recv.at[2, src], (q, mych),
+            ),
+        )
+
+    def mix_copy(q, src):
+        return send_to(
+            proj.at[1:3, :, lanes_of(q)], pin.at[1:3, tile(src), :],
+            in_send.at[1, q], in_recv.at[1, src], (q, mych),
+        )
+
+    def gate_copies(q, src):
+        return (
+            send_to(
+                proj.at[0:1, :, lanes_of(q)], pin.at[0:1, tile(src), :],
+                in_send.at[1, q], in_recv.at[1, src], (q, mych),
+            ),
+            near_copies(q, src)[1],
+        )
+
+    for q in everyone:
+        tap_copy(q, me).start()
+
+    @pl.when(me == hs - 1)
+    def _():
+        for q in far:
+            halo_copy(q, me, LANES - 16).start()
+
+    @pl.when(me == hs)
+    def _():
+        for q in far:
+            halo_copy(q, me, 0).start()
+
+    for i in range(hs):
+        @pl.when(half == 0)
+        def _():
+            mix_copy(far[i], me).start()
+
+        @pl.when(half == 1)
+        def _():
+            for copy in gate_copies(far[i], me):
+                copy.start()
+
+        if i < hs - 1:
+            for copy in near_copies(near[i], me):
+                copy.start()
+
+    taps[me] = tap_send[mine // group_owners]
+    gram[...] = jnp.zeros(gram.shape, jnp.float32)
+    for j in range(3):
+        for t in range(2):
+            wide[j, t, 0:8, :] = jnp.zeros((8, LANES), jnp.float32)
+            fgrad[j, t, span : span + 16, :] = jnp.zeros((16, LANES), jnp.float32)
+        for k in range(kt):
+            gs_acc[j, k] = jnp.zeros((8, WIDE), jnp.float32)
+    for q in everyone:
+        tap_copy(q, q).wait_recv()
+    build_filters(taps, ns, low_hi, low_lo, up_hi, up_lo)
+    for copy in own[1:]:
+        copy.wait()
+    halo_copy(far[0], 0, 0).wait_recv()
+
+    sides = [slice(0, LANES), slice(LANES, WIDE)]
+
+    def to_wide(j, first, rows):
+        for t, lanes in enumerate(sides):
+            wide[j, t, pl.ds(first + 8, rows), :] = pin[j, pl.ds(first, rows), lanes].astype(
+                jnp.float32
+            )
+
+    def feature(j, first, rows):
+        sums = []
+        for t, lanes in enumerate(sides):
+            acc = jnp.zeros((rows, LANES), jnp.float32)
+            for k in range(kt):
+                shifted = wide[j, t, pl.ds(first + 8 - k, rows), :]
+                acc = acc + weight[j, k : k + 1, lanes] * shifted
+            sums.append(acc)
+        return jnp.concatenate(sums, 1)
+
+    def keep(store, rows, value):
+        top, rest = split_halves(value)
+        store[rows, 0:WIDE] = top
+        store[rows, WIDE:] = rest
+
+    def near_block(i, carry):
+        b = half * hs + i
+
+        @pl.when(b != me)
+        def _():
+            for copy in near_copies(b, b):
+                copy.wait_recv()
+
+        base = pl.multiple_of(b * LANES, LANES)
+        for j in range(3):
+            to_wide(j, base, LANES)
+        def piece(p, carry):
+            first = pl.multiple_of(base + p * ROWS, ROWS)
+            rows = pl.ds(first, ROWS)
+            kept = pl.ds(pl.multiple_of(i * LANES + p * ROWS, ROWS), ROWS)
+            one, two = feature(1, first, ROWS), feature(2, first, ROWS)
+            feat[0, kept, :] = one
+            feat[1, kept, :] = two
+            keep(mixed, rows, one * two)
+            keep(gated, rows, cin[rows, :].astype(jnp.float32) * feature(0, first, ROWS))
+            return carry
+
+        return lax.fori_loop(0, LANES // ROWS, piece, carry)
+
+    def far_block(early, i, carry):
+        b = (1 - half) * hs + i
+        base = pl.multiple_of(b * LANES, LANES)
+        for copy in gate_copies(b, b) if early else (mix_copy(b, b),):
+            copy.wait_recv()
+        for j in (0,) if early else (1, 2):
+            to_wide(j, base, LANES)
+        def piece(p, carry):
+            first = pl.multiple_of(base + p * ROWS, ROWS)
+            rows = pl.ds(first, ROWS)
+            if early:
+                keep(gated, rows, cin[rows, :].astype(jnp.float32) * feature(0, first, ROWS))
+            else:
+                keep(mixed, rows, feature(1, first, ROWS) * feature(2, first, ROWS))
+            return carry
+
+        return lax.fori_loop(0, LANES // ROWS, piece, carry)
+
+    flip = (
+        lax.broadcasted_iota(jnp.int32, (WIDE, WIDE), 0)
+        + lax.broadcasted_iota(jnp.int32, (WIDE, WIDE), 1)
+        == WIDE - 1
+    ).astype(jnp.float32).astype(jnp.bfloat16)
+
+    def add_gram(pairs, lanes):
+        for b in sorted({b for b, _ in pairs}):
+            left = dot32(flip, mixed[b * WIDE : (b + 1) * WIDE, :]).astype(jnp.bfloat16)
+            left_top, left_rest = left[:, :WIDE][:, lanes], left[:, WIDE:][:, lanes]
+            for c in sorted(c for first, c in pairs if first == b):
+                right = gated[c * WIDE : (c + 1) * WIDE, :]
+                right_top, right_rest = right[:, :WIDE][:, lanes], right[:, WIDE:][:, lanes]
+                cols = slice((c - b) * WIDE, (c - b + 1) * WIDE)
+                gram[:, cols] += (
+                    dot32_t(left_top, right_top)
+                    + dot32_t(left_rest, right_top)
+                    + dot32_t(left_top, right_rest)
+                )
+
+    def conv_of(b, first, last, rows=WIDE):
+        start = total - (b + 1) * WIDE
+        cols = slice(start + first, start + last)
+        return dot_three(low_hi[:rows, cols], low_lo[:rows, cols], mixed[first:last, :])
+
+    def corr_of(a, first, last, rows=WIDE):
+        cols = slice(first - a * WIDE, last - a * WIDE)
+        return dot_three(up_hi[:rows, cols], up_lo[:rows, cols], gated[first:last, :])
+
+    def keep_grad(j, rows, value):
+        for t, lanes in enumerate(sides):
+            fgrad[j, t, rows, :] = value[:, lanes]
+
+    def grads_of(rows, conv=None, corr=None):
+        if conv is not None:
+            at = pl.ds(own_base + rows.start, rows.stop - rows.start)
+            keep_grad(0, rows, cin[at, :].astype(jnp.float32) * conv)
+        if corr is not None:
+            keep_grad(1, rows, corr * feat[1, rows, :])
+            keep_grad(2, rows, corr * feat[0, rows, :])
+
+    per = span // WIDE
+    local_rows = [slice(b * WIDE, (b + 1) * WIDE) for b in range(per)]
+    edge = slice(span, span + 16)
+    near_pairs = [(b, c) for b in range(per) for c in range(b, per)]
+    far_pairs = [(b, c) for b in range(per) for c in range(per, 2 * per)]
+
+    @pl.when(half == 0)
+    def _():
+        for j in (1, 2):
+            for t, lanes in enumerate(sides):
+                wide[j, t, 8 + span : 8 + span + 16, :] = halo[j, :, lanes].astype(jnp.float32)
+        lax.fori_loop(0, hs, near_block, 0)
+        mixed[span : span + LANES, :] = jnp.zeros((LANES, 2 * WIDE), jnp.bfloat16)
+        one, two = feature(1, span, 16), feature(2, span, 16)
+        feat[0, edge, :] = one
+        feat[1, edge, :] = two
+        keep(mixed, edge, one * two)
+        for b in range(per):
+            grads_of(local_rows[b], conv=conv_of(b, 0, (b + 1) * WIDE))
+            part[local_rows[b], :] = corr_of(b, b * WIDE, span)
+        part_edge[...] = conv_of(per, 0, span + LANES, 16)
+        add_gram(near_pairs, slice(0, WIDE))
+        lax.fori_loop(0, hs, functools.partial(far_block, True), 0)
+        for b in range(per):
+            grads_of(local_rows[b], corr=part[local_rows[b], :] + corr_of(b, span, total))
+        grads_of(edge, conv=part_edge[...], corr=corr_of(per, span, total, 16))
+
+    @pl.when(half == 1)
+    def _():
+        for j in range(3):
+            for t, lanes in enumerate(sides):
+                wide[j, t, 8 + span - 16 : 8 + span, :] = halo[j, :, lanes].astype(jnp.float32)
+        lax.fori_loop(0, hs, near_block, 0)
+        for b in range(per):
+            grads_of(local_rows[b], corr=corr_of(per + b, span + b * WIDE, total))
+            part[local_rows[b], :] = conv_of(per + b, span, span + (b + 1) * WIDE)
+        add_gram([(per + b, per + c) for b, c in near_pairs], slice(0, WIDE))
+        lax.fori_loop(0, hs, functools.partial(far_block, False), 0)
+        for b in range(per):
+            grads_of(local_rows[b], conv=part[local_rows[b], :] + conv_of(per + b, 0, span))
+
+    def finish_block(i, carry):
+        b = lax.rem(mine + 1 + i, hs)
+        base = pl.multiple_of(b * LANES, LANES)
+
+        def piece(p, carry):
+            first = pl.multiple_of(base + p * ROWS, ROWS)
+            for j in range(3):
+                for t, lanes in enumerate(sides):
+                    acc = jnp.zeros((ROWS, LANES), jnp.float32)
+                    source = wide[j, t, pl.ds(own_base + first + 8, ROWS), :]
+                    for k in range(kt):
+                        shifted = fgrad[j, t, pl.ds(first + k, ROWS), :]
+                        acc = acc + weight[j, k : k + 1, lanes] * shifted
+                        terms = (shifted * source).reshape(ROWS // 8, 8, LANES)
+                        gs_acc[j, k, :, lanes] += jnp.sum(terms, 0)
+                    gp_send[j, pl.ds(first, ROWS), lanes] = acc.astype(jnp.bfloat16)
+            return carry
+
+        lax.fori_loop(0, LANES // ROWS, piece, 0)
+
+        @pl.when(b != mine)
+        def _():
+            q = half * hs + b
+            send_to(
+                gp_send.at[:, tile(b), :], gp_out.at[:, :, lanes_of(me)],
+                gp_ssem.at[q], gp_rsem.at[me], (q, mych),
+            ).start()
+
+        return carry
+
+    lax.fori_loop(0, hs, finish_block, 0)
+
+    short_scale = 1.0 / math.sqrt(total)
+    for j in range(3):
+        lines = [jnp.sum(gs_acc[j, k], 0, keepdims=True) for k in range(kt)]
+        lines += [jnp.zeros((1, WIDE), jnp.float32)] * (8 - kt)
+        gs_send[j] = jnp.concatenate(lines, 0) * short_scale
+    partner = far[0]
+    pair = send_to(gs_send, gs_pair, pair_sem.at[0], pair_sem.at[1], (partner, mych))
+    pair.start()
+    gp_out[:, :, lanes_of(me)] = gp_send[:, tile(mine), :]
+
+    @pl.when(half == 0)
+    def _():
+        add_gram(far_pairs, slice(0, LANES))
+
+    @pl.when(half == 1)
+    def _():
+        add_gram(far_pairs, slice(LANES, WIDE))
+
+    filter_scale = 1.0 / math.sqrt(total * group_owners * WIDE)
+    for d, line in enumerate(diagonal_sums(gram, ns)):
+        fa_send[d] = jnp.broadcast_to(line * filter_scale, (8, LANES))
+    fa_copy = lambda q, src: send_to(
+        fa_send.at[q], fa_recv.at[src], fa_ssem.at[q], fa_rsem.at[src], (q, mych)
+    )
+    for q in everyone:
+        fa_copy(q, me).start()
+    fa_recv[me] = fa_send[me]
+
+    pair.wait()
+    gs_sum[...] = gs_send[...] + gs_pair[...]
+    gs_copy = lambda q, src: send_to(
+        gs_sum, gs_recv.at[lax.rem(src, hs)], gs_ssem.at[q], gs_rsem.at[src], (q, mych)
+    )
+    for q in near:
+        gs_copy(q, me).start()
+    gs_recv[mine] = gs_sum[...]
+
+    for q in everyone:
+        fa_copy(q, q).wait_recv()
+    for g in range(groups):
+        owners = [h * hs + g * group_owners + i for h in range(2) for i in range(group_owners)]
+        summed = fa_recv[owners[0]]
+        for q in owners[1:]:
+            summed = summed + fa_recv[q]
+        fb_send[g] = summed
+    fb_copy = lambda c, src: send_to(
+        fb_send, fb_recv.at[src], fb_ssem.at[c], fb_rsem.at[src], (me, c)
+    )
+    for _, c in ch_peers:
+        fb_copy(c, mych).start()
+    fb_recv[mych] = fb_send[...]
+    for _, c in ch_peers:
+        fb_copy(c, c).wait_recv()
+    width = LANES // nc
+    for c in range(nc):
+        for g in range(groups):
+            line = fb_recv[c, g]
+            piece = line[:, 0:width]
+            for other in range(1, nc):
+                piece = jnp.where(
+                    mych == other, line[:, other * width : (other + 1) * width], piece
+                )
+            at = c * groups + g
+            gf_out[at : at + 1, :] = piece[0:1, :]
+
+    for q in near:
+        gs_copy(q, q).wait_recv()
+    for q in range(hs):
+        for j in range(3):
+            gs_out[j, :, q * WIDE : (q + 1) * WIDE] = gs_recv[q, j, 0:kt, :]
+
+    for q in everyone:
+        tap_copy(q, me).wait_send()
+        fa_copy(q, me).wait_send()
+    for q in near:
+        for copy in near_copies(q, me):
+            copy.wait_send()
+        gs_copy(q, me).wait_send()
+        send_to(
+            gp_send.at[:, tile(lax.rem(q, hs)), :], gp_out.at[:, :, lanes_of(q)],
+            gp_ssem.at[q], gp_rsem.at[q], (q, mych),
+        ).wait()
+    for _, c in ch_peers:
+        fb_copy(c, mych).wait_send()
+
+    @pl.when(half == 0)
+    def _():
+        for q in far:
+            mix_copy(q, me).wait_send()
+
+    @pl.when(half == 1)
+    def _():
+        for q in far:
+            for copy in gate_copies(q, me):
+                copy.wait_send()
+
+    @pl.when((me == hs - 1) | (me == hs))
+    def _():
+        for q in far:
+            halo_copy(q, me, 0).wait_send()
+
+
+def resident(projected, cotangent, short_weight, long_filter):
+    row_count, streams, chan_count = projected.shape
+    kt = short_weight.shape[1]
+    groups = long_filter.shape[0]
+    ns, nc = lax.axis_size("seq"), lax.axis_size("ch")
+    total = row_count * ns
+    span = total // 2
+    f32, bf16 = jnp.float32, jnp.bfloat16
+    dma = pltpu.SemaphoreType.DMA
+    vmem = pl.BlockSpec(memory_space=pltpu.VMEM)
+    anywhere = pl.BlockSpec(memory_space=pl.ANY)
+    grad_proj, grad_short, grad_filter = pl.pallas_call(
+        functools.partial(resident_kernel, ns, nc, kt, groups),
+        out_shape=(
+            jax.ShapeDtypeStruct((streams, row_count, chan_count), bf16),
+            jax.ShapeDtypeStruct((streams, kt, chan_count), f32),
+            jax.ShapeDtypeStruct((groups * nc, row_count // nc), f32),
+        ),
+        in_specs=[anywhere] * 4,
+        out_specs=(vmem, vmem, vmem),
+        scratch_shapes=[
+            pltpu.VMEM((3, kt, WIDE), f32),
+            pltpu.VMEM((groups, LANES), f32),
+            pltpu.VMEM((3, total, WIDE), bf16),
+            pltpu.VMEM((total, WIDE), bf16),
+            pltpu.VMEM((3, 16, WIDE), bf16),
+            pltpu.VMEM((3, 2, total + 8, LANES), f32),
+            pltpu.VMEM((2, span + 16, WIDE), f32),
+            pltpu.VMEM((total, 2 * WIDE), bf16),
+            pltpu.VMEM((total, 2 * WIDE), bf16),
+            pltpu.VMEM((span, WIDE), f32),
+            pltpu.VMEM((16, WIDE), f32),
+            pltpu.VMEM((3, 2, span + 16, LANES), f32),
+            pltpu.VMEM((3, span, WIDE), bf16),
+            pltpu.VMEM((groups, 8, LANES), f32),
+            pltpu.VMEM((ns, 8, LANES), f32),
+            pltpu.VMEM((WIDE, total), bf16),
+            pltpu.VMEM((WIDE, total), bf16),
+            pltpu.VMEM((WIDE, total), bf16),
+            pltpu.VMEM((WIDE, total), bf16),
+            pltpu.VMEM((WIDE, total), f32),
+            pltpu.VMEM((ns, 8, LANES), f32),
+            pltpu.VMEM((ns, 8, LANES), f32),
+            pltpu.VMEM((groups, 8, LANES), f32),
+            pltpu.VMEM((nc, groups, 8, LANES), f32),
+            pltpu.VMEM((3, 8, 8, WIDE), f32),
+            pltpu.VMEM((3, 8, WIDE), f32),
+            pltpu.VMEM((3, 8, WIDE), f32),
+            pltpu.VMEM((3, 8, WIDE), f32),
+            pltpu.VMEM((ns // 2, 3, 8, WIDE), f32),
+            dma((4,)),
+            dma((4, ns)), dma((4, ns)),
+            dma((ns,)), dma((ns,)),
+            dma((ns,)), dma((ns,)),
+            dma((ns,)), dma((ns,)),
+            dma((nc,)), dma((nc,)),
+            dma((2,)),
+        ],
+        compiler_params=pltpu.CompilerParams(
+            collective_id=0, has_side_effects=True, vmem_limit_bytes=48 * 1024 * 1024
+        ),
+    )(jnp.transpose(projected, (1, 0, 2)), cotangent, short_weight, long_filter)
+    return jnp.transpose(grad_proj, (1, 0, 2)), grad_short, grad_filter
+
+
+def spread(projected, cotangent, short_weight, long_filter):
     tap_count = short_weight.shape[1]
     row_count = projected.shape[0]
     margin = tap_count - 1
@@ -174,6 +739,21 @@
     return (grad_proj.astype(jnp.bfloat16), grad_short, owned_grad)
 
 
+def local(projected, cotangent, short_weight, long_filter):
+    row_count, _, chan_count = projected.shape
+    seq_count = lax.axis_size("seq")
+    group_width = chan_count // long_filter.shape[0]
+    fits = (
+        row_count == LANES
+        and seq_count % 4 == 0
+        and chan_count == WIDE * (seq_count // 2)
+        and group_width % WIDE == 0
+        and short_weight.shape[1] <= 8
+    )
+    plan = resident if fits else spread
+    return plan(projected, cotangent, short_weight, long_filter)
+
+
 def solution(mesh):
     return jax.shard_map(
         local,

time: 399 us -> 57.3 us (0.14)
  waiting for transfers between devices: 258 us -> 0 us
  Pallas kernels: 0 us -> 50.6 us
  starting transfers between devices: 44.4 us -> 0 us
  local copies, waits for them, and re-layouts: 45 us -> 5.76 us
  other arithmetic: 20.5 us -> 0 us
  matrix products: 15.2 us -> 0 us
  between operations: 14.7 us -> 0.65 us
    all_to_all x9 -> x0, waiting for transfers between devices: 191 us -> none  [the longest x4 185 us: transpose_pair(): lax.all_to_all(signals, 'seq', split_axis=0, concat_axis=1, tiled=True)]
    psum x1 -> x0, waiting for transfers between devices: 63.5 us -> none  [local(): lax.psum(jnp.stack(short_terms, 1), 'seq') * (1.0 / math.sqrt(token_count))]
    pallas_call x0 -> x1, Pallas kernels: none -> 50.6 us  [resident(): pl.pallas_call(functools.partial(resident_kernel, ns, nc, kt, groups), ou...]
    all_to_all x9 -> x0, starting transfers between devices: 38.2 us -> none  [the longest x4 19 us: transpose_pair(): lax.all_to_all(signals, 'seq', split_axis=0, concat_axis=1, tiled=True)]
    dot_general x11 -> x0, matrix products: 15.2 us -> none  [the longest x5 9.44 us: complex_dft(): result = jnp.einsum(joined, table, stacked, precision=highest)]
    all_to_all x12 -> x0, local copies, waits for them, and re-layouts: 11.6 us -> none  [the longest x5 9.88 us: transpose_pair(): lax.all_to_all(signals, 'seq', split_axis=0, concat_axis=1, tiled=True)]
    unnamed x42 -> x11, local copies, waits for them, and re-layouts: 14.9 us -> 5.76 us
    another operation x8 -> x0, local copies, waits for them, and re-layouts: 8.77 us -> none  [the longest x1 5.24 us: sequence_plan(): jnp.stack([sig_re, sig_im], 2)]
  transfers between devices with their start and end apart: 12 -> 0, of which waited for: 8 -> 0; matrix products, arithmetic and copies ran while one was open for 10% -> 0% of each run, Pallas kernels for 0% -> 0%
where the time goes in v2:
time: 57.3 us; the launch traced here: 57 us
  Pallas kernels  50.6 us (88%)
  local copies, waits for them, and re-layouts  5.76 us (10%)
  between operations  0.65 us (1%)
    pallas_call x1, Pallas kernels, resident(): pl.pallas_call(functools.partial(resident_kernel, ns, nc, kt, groups), ou...  50.6 us
    unnamed x11, local copies, waits for them, and re-layouts  5.76 us

profile of v2, /device:TPU:0, one launch (start us, length us, event | category | flops | bytes accessed | tf_op | source)
XLA Modules:
  0.0 57.0 jit_solution(1683698364455455285)
XLA Ops:
  0.6 0.0 copy-start.3
  0.6 0.7 %copy-done.3 = f32[2,128]{1,0:T(2,128)S(1)} copy-done((f32[2,128]{1,0:T(2,128)S(1)}, f32[2,128]{1,0:T(2,128)}, u32[]{:S(2)}) %copy-start.3) | copy-done | bytes 1048
  1.3 0.0 copy-start
  1.3 1.1 %copy-done = bf16[128,3,1024]{2,0,1:T(8,128)(2,1)S(1)} copy-done((bf16[128,3,1024]{2,0,1:T(8,128)(2,1)S(1)}, bf16[128,3,1024]{2,0,1:T(8,128)(2,1)}, u32[]{:S(2)}) %copy-start) | copy-done | bytes 786456
  2.4 0.0 copy-start.1
  2.4 0.9 %copy-done.1 = bf16[128,1024]{1,0:T(8,128)(2,1)S(1)} copy-done((bf16[128,1024]{1,0:T(8,128)(2,1)S(1)}, bf16[128,1024]{1,0:T(8,128)(2,1)}, u32[]{:S(2)}) %copy-start.1) | copy-done | bytes 262168
  3.4 0.0 copy-start.2
  3.4 0.9 %copy-done.2 = f32[3,7,1024]{2,1,0:T(8,128)S(1)} copy-done((f32[3,7,1024]{2,1,0:T(8,128)S(1)}, f32[3,7,1024]{2,1,0:T(8,128)}, u32[]{:S(2)}) %copy-start.2) | copy-done | bytes 86040
  4.3 50.6 %shard_map.67 = (bf16[3,128,1024]{2,1,0:T(8,128)(2,1)S(1)}, f32[3,7,1024]{2,1,0:T(8,128)S(1)}, f32[8,32]{1,0:T(8,128)S(1)}) custom-call(bf16[3,128,1024]{2,1,0:T(8,128)(2,1)S(1)} %bitcast.3, bf16[128,1024]{1,0:T(8,128)(2,1)S(1)} %copy-done.1, f32[3,7,1024]{2,1,0:T(8,128)S(1)} %copy-done.2, f32[2,128]{1,0:T(2,128)S(1)} %copy-done.3), custom_call_target="tpu_custom_call" | custom-call | tf_op jit(solution)/shard_map/pallas_call | solution.py:653
  54.9 0.9 %copy.10 = bf16[128,3,1024]{2,0,1:T(8,128)(2,1)} copy(bf16[128,3,1024]{2,0,1:T(8,128)(2,1)S(1)} %bitcast.2) | data formatting | bytes 1572864
  55.8 0.6 %copy.11 = f32[3,7,1024]{2,1,0:T(8,128)} copy(f32[3,7,1024]{2,1,0:T(8,128)S(1)} %get-tuple-element.13) | data formatting | bytes 172032
  56.4 0.6 %copy.12 = f32[8,32]{1,0:T(8,128)} copy(f32[8,32]{1,0:T(8,128)S(1)} %get-tuple-element.14) | data formatting | bytes 2048
Async XLA Ops:
  0.6 0.7 %copy-start.3 = (f32[2,128]{1,0:T(2,128)S(1)}, f32[2,128]{1,0:T(2,128)}, u32[]{:S(2)}) copy-start(f32[2,128]{1,0:T(2,128)} %filt_in.1) | copy-start | bytes 3076
  1.3 1.1 %copy-start = (bf16[128,3,1024]{2,0,1:T(8,128)(2,1)S(1)}, bf16[128,3,1024]{2,0,1:T(8,128)(2,1)}, u32[]{:S(2)}) copy-start(bf16[128,3,1024]{2,0,1:T(8,128)(2,1)} %param.4) | copy-start | bytes 2359300
  2.4 0.9 %copy-start.1 = (bf16[128,1024]{1,0:T(8,128)(2,1)S(1)}, bf16[128,1024]{1,0:T(8,128)(2,1)}, u32[]{:S(2)}) copy-start(bf16[128,1024]{1,0:T(8,128)(2,1)} %cot.1) | copy-start | bytes 786436
  3.4 0.9 %copy-start.2 = (f32[3,7,1024]{2,1,0:T(8,128)S(1)}, f32[3,7,1024]{2,1,0:T(8,128)}, u32[]{:S(2)}) copy-start(f32[3,7,1024]{2,1,0:T(8,128)} %weight_in.1) | copy-start | bytes 258052

commit v3 on v2

--- a/solution.py
+++ b/solution.py
@@ -241,7 +241,7 @@
     weight, filt, pin, cin, halo, wide, feat, mixed, gated, part, part_edge, fgrad, gp_send,
     tap_send, taps, low_hi, low_lo, up_hi, up_lo, gram,
     fa_send, fa_recv, fb_send, fb_recv, gs_acc, gs_send, gs_pair, gs_sum, gs_recv,
-    local_sem, in_send, in_recv, gp_ssem, gp_rsem, gs_ssem, gs_rsem,
+    local_sem, tap_ssem, tap_rsem, in_send, in_recv, gp_ssem, gp_rsem, gs_ssem, gs_rsem,
     fa_ssem, fa_rsem, fb_ssem, fb_rsem, pair_sem,
 ):
     me = lax.axis_index("seq")
@@ -257,14 +257,22 @@
     far = [(1 - half) * hs + lax.rem(mine + i, hs) for i in range(hs)]
     everyone = near + far
     ch_peers = [(me, lax.rem(mych + i, nc)) for i in range(1, nc)]
-    lanes_of = lambda q: tile(lax.rem(q, hs), WIDE)
+    lanes_of = lambda q, t: tile(lax.rem(q, hs) * 2 + t)
 
     own = [
         pltpu.make_async_copy(filt_in, filt, local_sem.at[0]),
-        pltpu.make_async_copy(weight_in.at[:, :, lanes_of(me)], weight, local_sem.at[1]),
-        pltpu.make_async_copy(proj.at[:, :, lanes_of(me)], pin.at[:, tile(me), :], local_sem.at[2]),
-        pltpu.make_async_copy(cot.at[:, lanes_of(me)], cin.at[tile(me), :], local_sem.at[3]),
     ]
+    for t in range(2):
+        lanes, at = lanes_of(me, t), tile(me)
+        own += [
+            pltpu.make_async_copy(
+                weight_in.at[:, :, lanes], weight.at[t], local_sem.at[1 + 3 * t]
+            ),
+            pltpu.make_async_copy(
+                proj.at[:, :, lanes], pin.at[t, :, at, :], local_sem.at[2 + 3 * t]
+            ),
+            pltpu.make_async_copy(cot.at[:, lanes], cin.at[t, at, :], local_sem.at[3 + 3 * t]),
+        ]
     for copy in own:
         copy.start()
     barrier = pltpu.get_barrier_semaphore()
@@ -280,148 +288,134 @@
     def tap_copy(q, src):
         return send_to(
             tap_send.at[lax.rem(q, hs) // group_owners], taps.at[src],
-            in_send.at[0, q], in_recv.at[0, src], (q, mych),
+            tap_ssem.at[q], tap_rsem.at[src], (q, mych),
         )
 
-    def halo_copy(q, src, first):
+    def halo_copy(q, t, src, first):
         return send_to(
-            proj.at[:, pl.ds(first, 16), lanes_of(q)], halo,
-            in_send.at[3, q], in_recv.at[3, 0], (q, mych),
+            proj.at[:, pl.ds(first, 16), lanes_of(q, t)], halo.at[t],
+            in_send.at[t, 2, q], in_recv.at[t, 2, 0], (q, mych),
         )
 
-    def near_copies(q, src):
-        return (
-            send_to(
-                proj.at[:, :, lanes_of(q)], pin.at[:, tile(src), :],
-                in_send.at[1, q], in_recv.at[1, src], (q, mych),
-            ),
-            send_to(
-                cot.at[:, lanes_of(q)], cin.at[tile(src), :],
-                in_send.at[2, q], in_recv.at[2, src], (q, mych),
-            ),
+    def stream_copy(q, t, src, streams):
+        return send_to(
+            proj.at[streams, :, lanes_of(q, t)], pin.at[t, streams, tile(src), :],
+            in_send.at[t, 0, q], in_recv.at[t, 0, src], (q, mych),
         )
 
-    def mix_copy(q, src):
+    def cot_copy(q, t, src):
         return send_to(
-            proj.at[1:3, :, lanes_of(q)], pin.at[1:3, tile(src), :],
-            in_send.at[1, q], in_recv.at[1, src], (q, mych),
+            cot.at[:, lanes_of(q, t)], cin.at[t, tile(src), :],
+            in_send.at[t, 1, q], in_recv.at[t, 1, src], (q, mych),
         )
 
-    def gate_copies(q, src):
-        return (
-            send_to(
-                proj.at[0:1, :, lanes_of(q)], pin.at[0:1, tile(src), :],
-                in_send.at[1, q], in_recv.at[1, src], (q, mych),
-            ),
-            near_copies(q, src)[1],
-        )
+    def near_copies(q, t, src):
+        return (stream_copy(q, t, src, slice(0, 3)), cot_copy(q, t, src))
+
+    def mix_copy(q, t, src):
+        return stream_copy(q, t, src, slice(1, 3))
+
+    def gate_copies(q, t, src):
+        return (stream_copy(q, t, src, slice(0, 1)), cot_copy(q, t, src))
 
     for q in everyone:
         tap_copy(q, me).start()
 
     @pl.when(me == hs - 1)
     def _():
-        for q in far:
-            halo_copy(q, me, LANES - 16).start()
+        for t in range(2):
+            for q in far:
+                halo_copy(q, t, me, LANES - 16).start()
 
     @pl.when(me == hs)
     def _():
-        for q in far:
-            halo_copy(q, me, 0).start()
-
-    for i in range(hs):
-        @pl.when(half == 0)
-        def _():
-            mix_copy(far[i], me).start()
-
-        @pl.when(half == 1)
-        def _():
-            for copy in gate_copies(far[i], me):
-                copy.start()
-
-        if i < hs - 1:
-            for copy in near_copies(near[i], me):
-                copy.start()
+        for t in range(2):
+            for q in far:
+                halo_copy(q, t, me, 0).start()
+
+    for t in range(2):
+        for i in range(hs):
+            @pl.when(half == 0)
+            def _():
+                mix_copy(far[i], t, me).start()
+
+            @pl.when(half == 1)
+            def _():
+                for copy in gate_copies(far[i], t, me):
+                    copy.start()
+
+            if i < hs - 1:
+                for copy in near_copies(near[i], t, me):
+                    copy.start()
 
     taps[me] = tap_send[mine // group_owners]
     gram[...] = jnp.zeros(gram.shape, jnp.float32)
     for j in range(3):
+        wide[j, 0:8, :] = jnp.zeros((8, LANES), jnp.float32)
+        fgrad[j, span : span + 16, :] = jnp.zeros((16, LANES), jnp.float32)
         for t in range(2):
-            wide[j, t, 0:8, :] = jnp.zeros((8, LANES), jnp.float32)
-            fgrad[j, t, span : span + 16, :] = jnp.zeros((16, LANES), jnp.float32)
-        for k in range(kt):
-            gs_acc[j, k] = jnp.zeros((8, WIDE), jnp.float32)
+            for k in range(kt):
+                gs_acc[t, j, k] = jnp.zeros((8, LANES), jnp.float32)
     for q in everyone:
         tap_copy(q, q).wait_recv()
     build_filters(taps, ns, low_hi, low_lo, up_hi, up_lo)
     for copy in own[1:]:
         copy.wait()
-    halo_copy(far[0], 0, 0).wait_recv()
-
-    sides = [slice(0, LANES), slice(LANES, WIDE)]
-
-    def to_wide(j, first, rows):
-        for t, lanes in enumerate(sides):
-            wide[j, t, pl.ds(first + 8, rows), :] = pin[j, pl.ds(first, rows), lanes].astype(
-                jnp.float32
-            )
-
-    def feature(j, first, rows):
-        sums = []
-        for t, lanes in enumerate(sides):
-            acc = jnp.zeros((rows, LANES), jnp.float32)
-            for k in range(kt):
-                shifted = wide[j, t, pl.ds(first + 8 - k, rows), :]
-                acc = acc + weight[j, k : k + 1, lanes] * shifted
-            sums.append(acc)
-        return jnp.concatenate(sums, 1)
+    for t in range(2):
+        halo_copy(far[0], t, 0, 0).wait_recv()
+
+    def to_wide(t, j, first):
+        wide[j, pl.ds(first + 8, LANES), :] = pin[t, j, pl.ds(first, LANES), :].astype(jnp.float32)
+
+    def feature(t, j, first, rows):
+        acc = jnp.zeros((rows, LANES), jnp.float32)
+        for k in range(kt):
+            acc = acc + weight[t, j, k : k + 1, :] * wide[j, pl.ds(first + 8 - k, rows), :]
+        return acc
 
     def keep(store, rows, value):
         top, rest = split_halves(value)
-        store[rows, 0:WIDE] = top
-        store[rows, WIDE:] = rest
-
-    def near_block(i, carry):
+        store[rows, 0:LANES] = top
+        store[rows, LANES:] = rest
+
+    def near_block(t, i, carry):
         b = half * hs + i
 
         @pl.when(b != me)
         def _():
-            for copy in near_copies(b, b):
+            for copy in near_copies(b, t, b):
                 copy.wait_recv()
 
         base = pl.multiple_of(b * LANES, LANES)
         for j in range(3):
-            to_wide(j, base, LANES)
-        def piece(p, carry):
-            first = pl.multiple_of(base + p * ROWS, ROWS)
+            to_wide(t, j, base)
+        for p in range(LANES // ROWS):
+            first = base + p * ROWS
             rows = pl.ds(first, ROWS)
-            kept = pl.ds(pl.multiple_of(i * LANES + p * ROWS, ROWS), ROWS)
-            one, two = feature(1, first, ROWS), feature(2, first, ROWS)
+            kept = pl.ds(pl.multiple_of(i * LANES, LANES) + p * ROWS, ROWS)
+            one, two = feature(t, 1, first, ROWS), feature(t, 2, first, ROWS)
             feat[0, kept, :] = one
             feat[1, kept, :] = two
             keep(mixed, rows, one * two)
-            keep(gated, rows, cin[rows, :].astype(jnp.float32) * feature(0, first, ROWS))
-            return carry
-
-        return lax.fori_loop(0, LANES // ROWS, piece, carry)
-
-    def far_block(early, i, carry):
+            keep(gated, rows, cin[t, rows, :].astype(jnp.float32) * feature(t, 0, first, ROWS))
+        return carry
+
+    def far_block(early, t, i, carry):
         b = (1 - half) * hs + i
         base = pl.multiple_of(b * LANES, LANES)
-        for copy in gate_copies(b, b) if early else (mix_copy(b, b),):
+        for copy in gate_copies(b, t, b) if early else (mix_copy(b, t, b),):
             copy.wait_recv()
         for j in (0,) if early else (1, 2):
-            to_wide(j, base, LANES)
-        def piece(p, carry):
-            first = pl.multiple_of(base + p * ROWS, ROWS)
+            to_wide(t, j, base)
+        for p in range(LANES // ROWS):
+            first = base + p * ROWS
             rows = pl.ds(first, ROWS)
             if early:
-                keep(gated, rows, cin[rows, :].astype(jnp.float32) * feature(0, first, ROWS))
+                gate = feature(t, 0, first, ROWS)
+                keep(gated, rows, cin[t, rows, :].astype(jnp.float32) * gate)
             else:
-                keep(mixed, rows, feature(1, first, ROWS) * feature(2, first, ROWS))
-            return carry
-
-        return lax.fori_loop(0, LANES // ROWS, piece, carry)
+                keep(mixed, rows, feature(t, 1, first, ROWS) * feature(t, 2, first, ROWS))
+        return carry
 
     flip = (
         lax.broadcasted_iota(jnp.int32, (WIDE, WIDE), 0)
@@ -429,18 +423,15 @@
         == WIDE - 1
     ).astype(jnp.float32).astype(jnp.bfloat16)
 
-    def add_gram(pairs, lanes):
+    def add_gram(pairs):
         for b in sorted({b for b, _ in pairs}):
             left = dot32(flip, mixed[b * WIDE : (b + 1) * WIDE, :]).astype(jnp.bfloat16)
-            left_top, left_rest = left[:, :WIDE][:, lanes], left[:, WIDE:][:, lanes]
             for c in sorted(c for first, c in pairs if first == b):
                 right = gated[c * WIDE : (c + 1) * WIDE, :]
-                right_top, right_rest = right[:, :WIDE][:, lanes], right[:, WIDE:][:, lanes]
+                top = right[:, :LANES]
                 cols = slice((c - b) * WIDE, (c - b + 1) * WIDE)
-                gram[:, cols] += (
-                    dot32_t(left_top, right_top)
-                    + dot32_t(left_rest, right_top)
-                    + dot32_t(left_top, right_rest)
+                gram[:, cols] += dot32_t(left, jnp.concatenate([top, top], 1)) + dot32_t(
+                    left[:, :LANES], right[:, LANES:]
                 )
 
     def conv_of(b, first, last, rows=WIDE):
@@ -452,17 +443,13 @@
         cols = slice(first - a * WIDE, last - a * WIDE)
         return dot_three(up_hi[:rows, cols], up_lo[:rows, cols], gated[first:last, :])
 
-    def keep_grad(j, rows, value):
-        for t, lanes in enumerate(sides):
-            fgrad[j, t, rows, :] = value[:, lanes]
-
-    def grads_of(rows, conv=None, corr=None):
+    def grads_of(t, rows, conv=None, corr=None):
         if conv is not None:
             at = pl.ds(own_base + rows.start, rows.stop - rows.start)
-            keep_grad(0, rows, cin[at, :].astype(jnp.float32) * conv)
+            fgrad[0, rows, :] = cin[t, at, :].astype(jnp.float32) * conv
         if corr is not None:
-            keep_grad(1, rows, corr * feat[1, rows, :])
-            keep_grad(2, rows, corr * feat[0, rows, :])
+            fgrad[1, rows, :] = corr * feat[1, rows, :]
+            fgrad[2, rows, :] = corr * feat[0, rows, :]
 
     per = span // WIDE
     local_rows = [slice(b * WIDE, (b + 1) * WIDE) for b in range(per)]
@@ -470,90 +457,93 @@
     near_pairs = [(b, c) for b in range(per) for c in range(b, per)]
     far_pairs = [(b, c) for b in range(per) for c in range(per, 2 * per)]
 
-    @pl.when(half == 0)
-    def _():
+    def early_part(t):
         for j in (1, 2):
-            for t, lanes in enumerate(sides):
-                wide[j, t, 8 + span : 8 + span + 16, :] = halo[j, :, lanes].astype(jnp.float32)
-        lax.fori_loop(0, hs, near_block, 0)
-        mixed[span : span + LANES, :] = jnp.zeros((LANES, 2 * WIDE), jnp.bfloat16)
-        one, two = feature(1, span, 16), feature(2, span, 16)
+            wide[j, 8 + span : 8 + span + 16, :] = halo[t, j].astype(jnp.float32)
+        lax.fori_loop(0, hs, functools.partial(near_block, t), 0)
+        mixed[span : span + LANES, :] = jnp.zeros((LANES, WIDE), jnp.bfloat16)
+        one, two = feature(t, 1, span, 16), feature(t, 2, span, 16)
         feat[0, edge, :] = one
         feat[1, edge, :] = two
         keep(mixed, edge, one * two)
         for b in range(per):
-            grads_of(local_rows[b], conv=conv_of(b, 0, (b + 1) * WIDE))
+            grads_of(t, local_rows[b], conv=conv_of(b, 0, (b + 1) * WIDE))
             part[local_rows[b], :] = corr_of(b, b * WIDE, span)
         part_edge[...] = conv_of(per, 0, span + LANES, 16)
-        add_gram(near_pairs, slice(0, WIDE))
-        lax.fori_loop(0, hs, functools.partial(far_block, True), 0)
+        add_gram(near_pairs)
+        lax.fori_loop(0, hs, functools.partial(far_block, True, t), 0)
         for b in range(per):
-            grads_of(local_rows[b], corr=part[local_rows[b], :] + corr_of(b, span, total))
-        grads_of(edge, conv=part_edge[...], corr=corr_of(per, span, total, 16))
-
-    @pl.when(half == 1)
-    def _():
+            grads_of(t, local_rows[b], corr=part[local_rows[b], :] + corr_of(b, span, total))
+        grads_of(t, edge, conv=part_edge[...], corr=corr_of(per, span, total, 16))
+
+    def late_part(t):
         for j in range(3):
-            for t, lanes in enumerate(sides):
-                wide[j, t, 8 + span - 16 : 8 + span, :] = halo[j, :, lanes].astype(jnp.float32)
-        lax.fori_loop(0, hs, near_block, 0)
+            wide[j, 8 + span - 16 : 8 + span, :] = halo[t, j].astype(jnp.float32)
+        lax.fori_loop(0, hs, functools.partial(near_block, t), 0)
         for b in range(per):
-            grads_of(local_rows[b], corr=corr_of(per + b, span + b * WIDE, total))
+            grads_of(t, local_rows[b], corr=corr_of(per + b, span + b * WIDE, total))
             part[local_rows[b], :] = conv_of(per + b, span, span + (b + 1) * WIDE)
-        add_gram([(per + b, per + c) for b, c in near_pairs], slice(0, WIDE))
-        lax.fori_loop(0, hs, functools.partial(far_block, False), 0)
+        add_gram([(per + b, per + c) for b, c in near_pairs])
+        lax.fori_loop(0, hs, functools.partial(far_block, False, t), 0)
         for b in range(per):
-            grads_of(local_rows[b], conv=part[local_rows[b], :] + conv_of(per + b, 0, span))
-
-    def finish_block(i, carry):
+            grads_of(t, local_rows[b], conv=part[local_rows[b], :] + conv_of(per + b, 0, span))
+
+    def finish_block(t, i, carry):
         b = lax.rem(mine + 1 + i, hs)
         base = pl.multiple_of(b * LANES, LANES)
-
-        def piece(p, carry):
-            first = pl.multiple_of(base + p * ROWS, ROWS)
+        for p in range(LANES // ROWS):
+            first = base + p * ROWS
             for j in range(3):
-                for t, lanes in enumerate(sides):
-                    acc = jnp.zeros((ROWS, LANES), jnp.float32)
-                    source = wide[j, t, pl.ds(own_base + first + 8, ROWS), :]
-                    for k in range(kt):
-                        shifted = fgrad[j, t, pl.ds(first + k, ROWS), :]
-                        acc = acc + weight[j, k : k + 1, lanes] * shifted
-                        terms = (shifted * source).reshape(ROWS // 8, 8, LANES)
-                        gs_acc[j, k, :, lanes] += jnp.sum(terms, 0)
-                    gp_send[j, pl.ds(first, ROWS), lanes] = acc.astype(jnp.bfloat16)
-            return carry
-
-        lax.fori_loop(0, LANES // ROWS, piece, 0)
+                acc = jnp.zeros((ROWS, LANES), jnp.float32)
+                source = wide[j, pl.ds(own_base + first + 8, ROWS), :]
+                for k in range(kt):
+                    shifted = fgrad[j, pl.ds(first + k, ROWS), :]
+                    acc = acc + weight[t, j, k : k + 1, :] * shifted
+                    terms = (shifted * source).reshape(ROWS // 8, 8, LANES)
+                    gs_acc[t, j, k] += jnp.sum(terms, 0)
+                gp_send[t, j, pl.ds(first, ROWS), :] = acc.astype(jnp.bfloat16)
 
         @pl.when(b != mine)
         def _():
-            q = half * hs + b
-            send_to(
-                gp_send.at[:, tile(b), :], gp_out.at[:, :, lanes_of(me)],
-                gp_ssem.at[q], gp_rsem.at[me], (q, mych),
-            ).start()
+            gp_copy(half * hs + b, t, me).start()
 
         return carry
 
-    lax.fori_loop(0, hs, finish_block, 0)
+    def gp_copy(q, t, src):
+        return send_to(
+            gp_send.at[t, :, tile(lax.rem(q, hs)), :], gp_out.at[:, :, lanes_of(src, t)],
+            gp_ssem.at[t, q], gp_rsem.at[t, src], (q, mych),
+        )
+
+    def one_tile(t, carry):
+        @pl.when(half == 0)
+        def _():
+            early_part(t)
+
+        @pl.when(half == 1)
+        def _():
+            late_part(t)
+
+        lax.fori_loop(0, hs, functools.partial(finish_block, t), 0)
+        gp_out[:, :, lanes_of(me, t)] = gp_send[t, :, tile(mine), :]
+
+        @pl.when(t == half)
+        def _():
+            add_gram(far_pairs)
+
+        return carry
+
+    lax.fori_loop(0, 2, one_tile, 0)
 
     short_scale = 1.0 / math.sqrt(total)
-    for j in range(3):
-        lines = [jnp.sum(gs_acc[j, k], 0, keepdims=True) for k in range(kt)]
-        lines += [jnp.zeros((1, WIDE), jnp.float32)] * (8 - kt)
-        gs_send[j] = jnp.concatenate(lines, 0) * short_scale
+    for t in range(2):
+        for j in range(3):
+            lines = [jnp.sum(gs_acc[t, j, k], 0, keepdims=True) for k in range(kt)]
+            lines += [jnp.zeros((1, LANES), jnp.float32)] * (8 - kt)
+            gs_send[t, j] = jnp.concatenate(lines, 0) * short_scale
     partner = far[0]
     pair = send_to(gs_send, gs_pair, pair_sem.at[0], pair_sem.at[1], (partner, mych))
     pair.start()
-    gp_out[:, :, lanes_of(me)] = gp_send[:, tile(mine), :]
-
-    @pl.when(half == 0)
-    def _():
-        add_gram(far_pairs, slice(0, LANES))
-
-    @pl.when(half == 1)
-    def _():
-        add_gram(far_pairs, slice(LANES, WIDE))
 
     filter_scale = 1.0 / math.sqrt(total * group_owners * WIDE)
     for d, line in enumerate(diagonal_sums(gram, ns)):
@@ -605,38 +595,42 @@
     for q in near:
         gs_copy(q, q).wait_recv()
     for q in range(hs):
-        for j in range(3):
-            gs_out[j, :, q * WIDE : (q + 1) * WIDE] = gs_recv[q, j, 0:kt, :]
+        for t in range(2):
+            lanes = slice((2 * q + t) * LANES, (2 * q + t + 1) * LANES)
+            for j in range(3):
+                gs_out[j, :, lanes] = gs_recv[q, t, j, 0:kt, :]
 
     for q in everyone:
         tap_copy(q, me).wait_send()
         fa_copy(q, me).wait_send()
     for q in near:
-        for copy in near_copies(q, me):
-            copy.wait_send()
         gs_copy(q, me).wait_send()
-        send_to(
-            gp_send.at[:, tile(lax.rem(q, hs)), :], gp_out.at[:, :, lanes_of(q)],
-            gp_ssem.at[q], gp_rsem.at[q], (q, mych),
-        ).wait()
+        for t in range(2):
+            for copy in near_copies(q, t, me):
+                copy.wait_send()
+            gp_copy(q, t, me).wait_send()
+            gp_copy(q, t, q).wait_recv()
     for _, c in ch_peers:
         fb_copy(c, mych).wait_send()
 
     @pl.when(half == 0)
     def _():
         for q in far:
-            mix_copy(q, me).wait_send()
+            for t in range(2):
+                mix_copy(q, t, me).wait_send()
 
     @pl.when(half == 1)
     def _():
         for q in far:
-            for copy in gate_copies(q, me):
-                copy.wait_send()
+            for t in range(2):
+                for copy in gate_copies(q, t, me):
+                    copy.wait_send()
 
     @pl.when((me == hs - 1) | (me == hs))
     def _():
         for q in far:
-            halo_copy(q, me, 0).wait_send()
+            for t in range(2):
+                halo_copy(q, t, me, 0).wait_send()
 
 
 def resident(projected, cotangent, short_weight, long_filter):
@@ -649,7 +643,7 @@
     f32, bf16 = jnp.float32, jnp.bfloat16
     dma = pltpu.SemaphoreType.DMA
     vmem = pl.BlockSpec(memory_space=pltpu.VMEM)
-    anywhere = pl.BlockSpec(memory_space=pl.ANY)
+    anywhere = pl.BlockSpec(memory_space=pltpu.HBM)
     grad_proj, grad_short, grad_filter = pl.pallas_call(
         functools.partial(resident_kernel, ns, nc, kt, groups),
         out_shape=(
@@ -660,19 +654,19 @@
         in_specs=[anywhere] * 4,
         out_specs=(vmem, vmem, vmem),
         scratch_shapes=[
-            pltpu.VMEM((3, kt, WIDE), f32),
+            pltpu.VMEM((2, 3, kt, LANES), f32),
             pltpu.VMEM((groups, LANES), f32),
-            pltpu.VMEM((3, total, WIDE), bf16),
+            pltpu.VMEM((2, 3, total, LANES), bf16),
+            pltpu.VMEM((2, total, LANES), bf16),
+            pltpu.VMEM((2, 3, 16, LANES), bf16),
+            pltpu.VMEM((3, total + 8, LANES), f32),
+            pltpu.VMEM((2, span + 16, LANES), f32),
             pltpu.VMEM((total, WIDE), bf16),
-            pltpu.VMEM((3, 16, WIDE), bf16),
-            pltpu.VMEM((3, 2, total + 8, LANES), f32),
-            pltpu.VMEM((2, span + 16, WIDE), f32),
-            pltpu.VMEM((total, 2 * WIDE), bf16),
-            pltpu.VMEM((total, 2 * WIDE), bf16),
-            pltpu.VMEM((span, WIDE), f32),
-            pltpu.VMEM((16, WIDE), f32),
-            pltpu.VMEM((3, 2, span + 16, LANES), f32),
-            pltpu.VMEM((3, span, WIDE), bf16),
+            pltpu.VMEM((total, WIDE), bf16),
+            pltpu.VMEM((span, LANES), f32),
+            pltpu.VMEM((16, LANES), f32),
+            pltpu.VMEM((3, span + 16, LANES), f32),
+            pltpu.VMEM((2, 3, span, LANES), bf16),
             pltpu.VMEM((groups, 8, LANES), f32),
             pltpu.VMEM((ns, 8, LANES), f32),
             pltpu.VMEM((WIDE, total), bf16),
@@ -684,21 +678,22 @@
             pltpu.VMEM((ns, 8, LANES), f32),
             pltpu.VMEM((groups, 8, LANES), f32),
             pltpu.VMEM((nc, groups, 8, LANES), f32),
-            pltpu.VMEM((3, 8, 8, WIDE), f32),
-            pltpu.VMEM((3, 8, WIDE), f32),
-            pltpu.VMEM((3, 8, WIDE), f32),
-            pltpu.VMEM((3, 8, WIDE), f32),
-            pltpu.VMEM((ns // 2, 3, 8, WIDE), f32),
-            dma((4,)),
-            dma((4, ns)), dma((4, ns)),
+            pltpu.VMEM((2, 3, 8, 8, LANES), f32),
+            pltpu.VMEM((2, 3, 8, LANES), f32),
+            pltpu.VMEM((2, 3, 8, LANES), f32),
+            pltpu.VMEM((2, 3, 8, LANES), f32),
+            pltpu.VMEM((ns // 2, 2, 3, 8, LANES), f32),
+            dma((7,)),
             dma((ns,)), dma((ns,)),
+            dma((2, 3, ns)), dma((2, 3, ns)),
+            dma((2, ns)), dma((2, ns)),
             dma((ns,)), dma((ns,)),
             dma((ns,)), dma((ns,)),
             dma((nc,)), dma((nc,)),
             dma((2,)),
         ],
         compiler_params=pltpu.CompilerParams(
-            collective_id=0, has_side_effects=True, vmem_limit_bytes=48 * 1024 * 1024
+            collective_id=0, has_side_effects=True, vmem_limit_bytes=56 * 1024 * 1024
         ),
     )(jnp.transpose(projected, (1, 0, 2)), cotangent, short_weight, long_filter)
     return jnp.transpose(grad_proj, (1, 0, 2)), grad_short, grad_filter

time: 57.3 us -> 51.6 us (0.901)
  Pallas kernels: 50.6 us -> 47.3 us
  local copies, waits for them, and re-layouts: 5.76 us -> 3.37 us
    pallas_call x1, Pallas kernels: 50.6 us -> 47.3 us  [resident(): pl.pallas_call(functools.partial(resident_kernel, ns, nc, kt, groups), ou...]
    unnamed x11 -> x7, local copies, waits for them, and re-layouts: 5.76 us -> 3.37 us
where the time goes in v3:
time: 51.6 us; the launch traced here: 51.3 us
  Pallas kernels  47.3 us (92%)
  local copies, waits for them, and re-layouts  3.37 us (7%)
  between operations  0.65 us (1%)
    pallas_call x1, Pallas kernels, resident(): pl.pallas_call(functools.partial(resident_kernel, ns, nc, kt, groups), ou...  47.3 us
    unnamed x7, local copies, waits for them, and re-layouts  3.37 us

profile of v3, /device:TPU:0, one launch (start us, length us, event | category | flops | bytes accessed | tf_op | source)
XLA Modules:
  0.0 51.3 jit_solution(7214445493354695765)
XLA Ops:
  0.6 47.3 %shard_map.67 = (bf16[3,128,1024]{2,1,0:T(8,128)(2,1)}, f32[3,7,1024]{2,1,0:T(8,128)}, f32[8,32]{1,0:T(8,128)}) custom-call(bf16[3,128,1024]{2,1,0:T(8,128)(2,1)} %bitcast.3, bf16[128,1024]{1,0:T(8,128)(2,1)} %cot.1, f32[3,7,1024]{2,1,0:T(8,128)} %weight_in.1, f32[2,128]{1,0:T(2,128)} %filt_in.1), custom_call_target="tpu_custom_call" | custom-call | tf_op jit(solution)/shard_map/pallas_call | solution.py:647
  48.0 0.0 copy-start
  48.0 2.1 %copy.10 = bf16[128,3,1024]{2,0,1:T(8,128)(2,1)} copy(bf16[128,3,1024]{2,0,1:T(8,128)(2,1)} %bitcast.2) | data formatting | bytes 1572864
  50.1 0.0 copy-done
  50.1 0.0 copy-start.1
  50.1 0.6 %copy.11 = f32[3,7,1024]{2,1,0:T(8,128)} copy(f32[3,7,1024]{2,1,0:T(8,128)S(1)} %copy-done) | data formatting | bytes 172032
  50.7 0.0 copy-done.1
  50.8 0.6 %copy.12 = f32[8,32]{1,0:T(8,128)} copy(f32[8,32]{1,0:T(8,128)S(1)} %copy-done.1) | data formatting | bytes 2048
Async XLA Ops:
  48.0 2.1 %copy-start = (f32[3,7,1024]{2,1,0:T(8,128)S(1)}, f32[3,7,1024]{2,1,0:T(8,128)}, u32[]{:S(2)}) copy-start(f32[3,7,1024]{2,1,0:T(8,128)} %get-tuple-element.13) | copy-start | bytes 258052
  50.1 0.7 %copy-start.1 = (f32[8,32]{1,0:T(8,128)S(1)}, f32[8,32]{1,0:T(8,128)}, u32[]{:S(2)}) copy-start(f32[8,32]{1,0:T(8,128)} %get-tuple-element.14) | copy-start | bytes 3076

commit v4 on v3

--- a/solution.py
+++ b/solution.py
@@ -503,7 +503,7 @@
                     gs_acc[t, j, k] += jnp.sum(terms, 0)
                 gp_send[t, j, pl.ds(first, ROWS), :] = acc.astype(jnp.bfloat16)
 
-        @pl.when(b != mine)
+        @pl.when(i < hs - 1)
         def _():
             gp_copy(half * hs + b, t, me).start()
 
@@ -515,6 +515,11 @@
             gp_ssem.at[t, q], gp_rsem.at[t, src], (q, mych),
         )
 
+    filter_scale = 1.0 / math.sqrt(total * group_owners * WIDE)
+    fa_copy = lambda q, src: send_to(
+        fa_send.at[q], fa_recv.at[src], fa_ssem.at[q], fa_rsem.at[src], (q, mych)
+    )
+
     def one_tile(t, carry):
         @pl.when(half == 0)
         def _():
@@ -524,13 +529,22 @@
         def _():
             late_part(t)
 
-        lax.fori_loop(0, hs, functools.partial(finish_block, t), 0)
-        gp_out[:, :, lanes_of(me, t)] = gp_send[t, :, tile(mine), :]
+        lax.fori_loop(0, hs - 1, functools.partial(finish_block, t), 0)
 
         @pl.when(t == half)
         def _():
             add_gram(far_pairs)
 
+        @pl.when(t == 1)
+        def _():
+            for d, line in enumerate(diagonal_sums(gram, ns)):
+                fa_send[d] = jnp.broadcast_to(line * filter_scale, (8, LANES))
+            for q in everyone:
+                fa_copy(q, me).start()
+            fa_recv[me] = fa_send[me]
+
+        finish_block(t, hs - 1, carry)
+        gp_out[:, :, lanes_of(me, t)] = gp_send[t, :, tile(mine), :]
         return carry
 
     lax.fori_loop(0, 2, one_tile, 0)
@@ -544,25 +558,6 @@
     partner = far[0]
     pair = send_to(gs_send, gs_pair, pair_sem.at[0], pair_sem.at[1], (partner, mych))
     pair.start()
-
-    filter_scale = 1.0 / math.sqrt(total * group_owners * WIDE)
-    for d, line in enumerate(diagonal_sums(gram, ns)):
-        fa_send[d] = jnp.broadcast_to(line * filter_scale, (8, LANES))
-    fa_copy = lambda q, src: send_to(
-        fa_send.at[q], fa_recv.at[src], fa_ssem.at[q], fa_rsem.at[src], (q, mych)
-    )
-    for q in everyone:
-        fa_copy(q, me).start()
-    fa_recv[me] = fa_send[me]
-
-    pair.wait()
-    gs_sum[...] = gs_send[...] + gs_pair[...]
-    gs_copy = lambda q, src: send_to(
-        gs_sum, gs_recv.at[lax.rem(src, hs)], gs_ssem.at[q], gs_rsem.at[src], (q, mych)
-    )
-    for q in near:
-        gs_copy(q, me).start()
-    gs_recv[mine] = gs_sum[...]
 
     for q in everyone:
         fa_copy(q, q).wait_recv()
@@ -578,6 +573,15 @@
     for _, c in ch_peers:
         fb_copy(c, mych).start()
     fb_recv[mych] = fb_send[...]
+    pair.wait()
+    gs_sum[...] = gs_send[...] + gs_pair[...]
+    gs_copy = lambda q, src: send_to(
+        gs_sum, gs_recv.at[lax.rem(src, hs)], gs_ssem.at[q], gs_rsem.at[src], (q, mych)
+    )
+    for q in near:
+        gs_copy(q, me).start()
+    gs_recv[mine] = gs_sum[...]
+
     for _, c in ch_peers:
         fb_copy(c, c).wait_recv()
     width = LANES // nc
@@ -644,6 +648,10 @@
     dma = pltpu.SemaphoreType.DMA
     vmem = pl.BlockSpec(memory_space=pltpu.VMEM)
     anywhere = pl.BlockSpec(memory_space=pltpu.HBM)
+    operands = [
+        pltpu.with_memory_space_constraint(x, pltpu.HBM)
+        for x in (jnp.transpose(projected, (1, 0, 2)), cotangent, short_weight, long_filter)
+    ]
     grad_proj, grad_short, grad_filter = pl.pallas_call(
         functools.partial(resident_kernel, ns, nc, kt, groups),
         out_shape=(
@@ -693,9 +701,9 @@
             dma((2,)),
         ],
         compiler_params=pltpu.CompilerParams(
-            collective_id=0, has_side_effects=True, vmem_limit_bytes=56 * 1024 * 1024
+            collective_id=0, has_side_effects=True, vmem_limit_bytes=48 * 1024 * 1024
         ),
-    )(jnp.transpose(projected, (1, 0, 2)), cotangent, short_weight, long_filter)
+    )(*operands)
     return jnp.transpose(grad_proj, (1, 0, 2)), grad_short, grad_filter
 
 

time: 51.6 us -> 49.3 us (0.955)
  local copies, waits for them, and re-layouts: 3.37 us -> 2.11 us
  Pallas kernels: 47.3 us -> 46.4 us
    unnamed x7 -> x3, local copies, waits for them, and re-layouts: 3.37 us -> 2.11 us
    pallas_call x1, Pallas kernels: 47.3 us -> 46.4 us  [resident(): pl.pallas_call(functools.partial(resident_kernel, ns, nc, kt, groups), ou...]
where the time goes in v4:
time: 49.3 us; the launch traced here: 49.1 us
  Pallas kernels  46.4 us (94%)
  local copies, waits for them, and re-layouts  2.11 us (4%)
  between operations  0.64 us (1%)
    pallas_call x1, Pallas kernels, resident(): pl.pallas_call(functools.partial(resident_kernel, ns, nc, kt, groups), ou...  46.4 us
    unnamed x3, local copies, waits for them, and re-layouts  2.11 us

profile of v4, /device:TPU:0, one launch (start us, length us, event | category | flops | bytes accessed | tf_op | source)
XLA Modules:
  0.0 49.1 jit_solution(11094186049251774129)
XLA Ops:
  0.6 46.4 %shard_map.67 = (bf16[3,128,1024]{2,1,0:T(8,128)(2,1)S(1)}, f32[3,7,1024]{2,1,0:T(8,128)S(1)}, f32[8,32]{1,0:T(8,128)S(1)}) custom-call(bf16[3,128,1024]{2,1,0:T(8,128)(2,1)} %bitcast.3, bf16[128,1024]{1,0:T(8,128)(2,1)} %cot.1, f32[3,7,1024]{2,1,0:T(8,128)} %weight_in.1, f32[2,128]{1,0:T(2,128)} %filt_in.1), custom_call_target="tpu_custom_call" | custom-call | tf_op jit(solution)/shard_map/pallas_call | solution.py:655
  47.0 0.9 %copy.10 = bf16[128,3,1024]{2,0,1:T(8,128)(2,1)} copy(bf16[128,3,1024]{2,0,1:T(8,128)(2,1)S(1)} %bitcast.2) | data formatting | bytes 1572864
  47.9 0.6 %copy.11 = f32[3,7,1024]{2,1,0:T(8,128)} copy(f32[3,7,1024]{2,1,0:T(8,128)S(1)} %get-tuple-element.13) | data formatting | bytes 172032
  48.5 0.6 %copy.12 = f32[8,32]{1,0:T(8,128)} copy(f32[8,32]{1,0:T(8,128)S(1)} %get-tuple-element.14) | data formatting | bytes 2048

commit v5 on v4

--- a/solution.py
+++ b/solution.py
@@ -238,10 +238,10 @@
     ns, nc, kt, groups,
     proj, cot, weight_in, filt_in,
     gp_out, gs_out, gf_out,
-    weight, filt, pin, cin, halo, wide, feat, mixed, gated, part, part_edge, fgrad, gp_send,
+    weight, filt, packed, pin, halo, wide, feat, mixed, gated, part, part_edge, fgrad, gp_send,
     tap_send, taps, low_hi, low_lo, up_hi, up_lo, gram,
     fa_send, fa_recv, fb_send, fb_recv, gs_acc, gs_send, gs_pair, gs_sum, gs_recv,
-    local_sem, tap_ssem, tap_rsem, in_send, in_recv, gp_ssem, gp_rsem, gs_ssem, gs_rsem,
+    local_sem, pack_sem, tap_ssem, tap_rsem, in_send, in_recv, gp_ssem, gp_rsem, gs_ssem, gs_rsem,
     fa_ssem, fa_rsem, fb_ssem, fb_rsem, pair_sem,
 ):
     me = lax.axis_index("seq")
@@ -263,16 +263,24 @@
         pltpu.make_async_copy(filt_in, filt, local_sem.at[0]),
     ]
     for t in range(2):
-        lanes, at = lanes_of(me, t), tile(me)
-        own += [
+        own.append(
             pltpu.make_async_copy(
-                weight_in.at[:, :, lanes], weight.at[t], local_sem.at[1 + 3 * t]
+                weight_in.at[:, :, lanes_of(me, t)], weight.at[t], local_sem.at[1 + t]
+            )
+        )
+    packs = []
+    for c in range(2 * hs):
+        lanes = slice(c * LANES, (c + 1) * LANES)
+        packs += [
+            pltpu.make_async_copy(
+                proj.at[1:3, :, lanes], packed.at[c, 0:2], pack_sem.at[0, c]
             ),
             pltpu.make_async_copy(
-                proj.at[:, :, lanes], pin.at[t, :, at, :], local_sem.at[2 + 3 * t]
+                proj.at[0:1, :, lanes], packed.at[c, 2:3], pack_sem.at[1, c]
             ),
-            pltpu.make_async_copy(cot.at[:, lanes], cin.at[t, at, :], local_sem.at[3 + 3 * t]),
+            pltpu.make_async_copy(cot.at[:, lanes], packed.at[c, 3], pack_sem.at[2, c]),
         ]
+    own += packs
     for copy in own:
         copy.start()
     barrier = pltpu.get_barrier_semaphore()
@@ -293,33 +301,29 @@
 
     def halo_copy(q, t, src, first):
         return send_to(
-            proj.at[:, pl.ds(first, 16), lanes_of(q, t)], halo.at[t],
-            in_send.at[t, 2, q], in_recv.at[t, 2, 0], (q, mych),
+            packed.at[lax.rem(q, hs) * 2 + t, 0:3, pl.ds(first, 16)], halo.at[t],
+            in_send.at[t, 1, q], in_recv.at[t, 1, 0], (q, mych),
         )
 
     def stream_copy(q, t, src, streams):
         return send_to(
-            proj.at[streams, :, lanes_of(q, t)], pin.at[t, streams, tile(src), :],
+            packed.at[lax.rem(q, hs) * 2 + t, streams], pin.at[t, src, streams],
             in_send.at[t, 0, q], in_recv.at[t, 0, src], (q, mych),
         )
 
-    def cot_copy(q, t, src):
-        return send_to(
-            cot.at[:, lanes_of(q, t)], cin.at[t, tile(src), :],
-            in_send.at[t, 1, q], in_recv.at[t, 1, src], (q, mych),
-        )
-
     def near_copies(q, t, src):
-        return (stream_copy(q, t, src, slice(0, 3)), cot_copy(q, t, src))
+        return (stream_copy(q, t, src, slice(0, 4)),)
 
     def mix_copy(q, t, src):
-        return stream_copy(q, t, src, slice(1, 3))
+        return stream_copy(q, t, src, slice(0, 2))
 
     def gate_copies(q, t, src):
-        return (stream_copy(q, t, src, slice(0, 1)), cot_copy(q, t, src))
+        return (stream_copy(q, t, src, slice(2, 4)),)
 
     for q in everyone:
         tap_copy(q, me).start()
+    for copy in packs:
+        copy.wait()
 
     @pl.when(me == hs - 1)
     def _():
@@ -359,13 +363,22 @@
     for q in everyone:
         tap_copy(q, q).wait_recv()
     build_filters(taps, ns, low_hi, low_lo, up_hi, up_lo)
-    for copy in own[1:]:
+    for copy in own[1:3]:
         copy.wait()
     for t in range(2):
+        pin[t, me] = packed[mine * 2 + t]
+    for t in range(2):
         halo_copy(far[0], t, 0, 0).wait_recv()
 
-    def to_wide(t, j, first):
-        wide[j, pl.ds(first + 8, LANES), :] = pin[t, j, pl.ds(first, LANES), :].astype(jnp.float32)
+    place = (2, 0, 1)
+
+    def to_wide(t, j, b):
+        first = pl.multiple_of(b * LANES, LANES)
+        block = pin[t, b, place[j]]
+        wide[j, pl.ds(first + 8, LANES), :] = block.astype(jnp.float32)
+
+    def cot_rows(t, b, first, rows):
+        return pin[t, b, 3, pl.ds(first, rows), :].astype(jnp.float32)
 
     def feature(t, j, first, rows):
         acc = jnp.zeros((rows, LANES), jnp.float32)
@@ -388,7 +401,7 @@
 
         base = pl.multiple_of(b * LANES, LANES)
         for j in range(3):
-            to_wide(t, j, base)
+            to_wide(t, j, b)
         for p in range(LANES // ROWS):
             first = base + p * ROWS
             rows = pl.ds(first, ROWS)
@@ -397,7 +410,7 @@
             feat[0, kept, :] = one
             feat[1, kept, :] = two
             keep(mixed, rows, one * two)
-            keep(gated, rows, cin[t, rows, :].astype(jnp.float32) * feature(t, 0, first, ROWS))
+            keep(gated, rows, cot_rows(t, b, p * ROWS, ROWS) * feature(t, 0, first, ROWS))
         return carry
 
     def far_block(early, t, i, carry):
@@ -406,13 +419,13 @@
         for copy in gate_copies(b, t, b) if early else (mix_copy(b, t, b),):
             copy.wait_recv()
         for j in (0,) if early else (1, 2):
-            to_wide(t, j, base)
+            to_wide(t, j, b)
         for p in range(LANES // ROWS):
             first = base + p * ROWS
             rows = pl.ds(first, ROWS)
             if early:
                 gate = feature(t, 0, first, ROWS)
-                keep(gated, rows, cin[t, rows, :].astype(jnp.float32) * gate)
+                keep(gated, rows, cot_rows(t, b, p * ROWS, ROWS) * gate)
             else:
                 keep(mixed, rows, feature(t, 1, first, ROWS) * feature(t, 2, first, ROWS))
         return carry
@@ -445,8 +458,10 @@
 
     def grads_of(t, rows, conv=None, corr=None):
         if conv is not None:
-            at = pl.ds(own_base + rows.start, rows.stop - rows.start)
-            fgrad[0, rows, :] = cin[t, at, :].astype(jnp.float32) * conv
+            size = min(rows.stop - rows.start, LANES)
+            blocks = range(rows.start // LANES, max(rows.stop // LANES, rows.start // LANES + 1))
+            grads = [cot_rows(t, half * hs + b, 0, size) for b in blocks]
+            fgrad[0, rows, :] = jnp.concatenate(grads, 0) * conv
         if corr is not None:
             fgrad[1, rows, :] = corr * feat[1, rows, :]
             fgrad[2, rows, :] = corr * feat[0, rows, :]
@@ -459,7 +474,7 @@
 
     def early_part(t):
         for j in (1, 2):
-            wide[j, 8 + span : 8 + span + 16, :] = halo[t, j].astype(jnp.float32)
+            wide[j, 8 + span : 8 + span + 16, :] = halo[t, place[j]].astype(jnp.float32)
         lax.fori_loop(0, hs, functools.partial(near_block, t), 0)
         mixed[span : span + LANES, :] = jnp.zeros((LANES, WIDE), jnp.bfloat16)
         one, two = feature(t, 1, span, 16), feature(t, 2, span, 16)
@@ -478,7 +493,7 @@
 
     def late_part(t):
         for j in range(3):
-            wide[j, 8 + span - 16 : 8 + span, :] = halo[t, j].astype(jnp.float32)
+            wide[j, 8 + span - 16 : 8 + span, :] = halo[t, place[j]].astype(jnp.float32)
         lax.fori_loop(0, hs, functools.partial(near_block, t), 0)
         for b in range(per):
             grads_of(t, local_rows[b], corr=corr_of(per + b, span + b * WIDE, total))
@@ -664,8 +679,8 @@
         scratch_shapes=[
             pltpu.VMEM((2, 3, kt, LANES), f32),
             pltpu.VMEM((groups, LANES), f32),
-            pltpu.VMEM((2, 3, total, LANES), bf16),
-            pltpu.VMEM((2, total, LANES), bf16),
+            pltpu.VMEM((ns, 4, LANES, LANES), bf16),
+            pltpu.VMEM((2, ns, 4, LANES, LANES), bf16),
             pltpu.VMEM((2, 3, 16, LANES), bf16),
             pltpu.VMEM((3, total + 8, LANES), f32),
             pltpu.VMEM((2, span + 16, LANES), f32),
@@ -691,9 +706,9 @@
             pltpu.VMEM((2, 3, 8, LANES), f32),
             pltpu.VMEM((2, 3, 8, LANES), f32),
             pltpu.VMEM((ns // 2, 2, 3, 8, LANES), f32),
-            dma((7,)),
+            dma((3,)), dma((3, ns)),
             dma((ns,)), dma((ns,)),
-            dma((2, 3, ns)), dma((2, 3, ns)),
+            dma((2, 2, ns)), dma((2, 2, ns)),
             dma((2, ns)), dma((2, ns)),
             dma((ns,)), dma((ns,)),
             dma((ns,)), dma((ns,)),

time: 49.3 us -> 49 us (level)
  no operation moved by 1% of the time
where the time goes in v5:
time: 49 us; the launch traced here: 48.9 us
  Pallas kernels  46.1 us (94%)
  local copies, waits for them, and re-layouts  2.11 us (4%)
  between operations  0.64 us (1%)
    pallas_call x1, Pallas kernels, resident(): pl.pallas_call(functools.partial(resident_kernel, ns, nc, kt, groups), ou...  46.1 us
    unnamed x3, local copies, waits for them, and re-layouts  2.11 us

profile of v5, /device:TPU:0, one launch (start us, length us, event | category | flops | bytes accessed | tf_op | source)
XLA Modules:
  0.0 48.9 jit_solution(1517378868289063573)
XLA Ops:
  0.6 46.1 %shard_map.67 = (bf16[3,128,1024]{2,1,0:T(8,128)(2,1)S(1)}, f32[3,7,1024]{2,1,0:T(8,128)S(1)}, f32[8,32]{1,0:T(8,128)S(1)}) custom-call(bf16[3,128,1024]{2,1,0:T(8,128)(2,1)} %bitcast.3, bf16[128,1024]{1,0:T(8,128)(2,1)} %cot.1, f32[3,7,1024]{2,1,0:T(8,128)} %weight_in.1, f32[2,128]{1,0:T(2,128)} %filt_in.1), custom_call_target="tpu_custom_call" | custom-call | tf_op jit(solution)/shard_map/pallas_call | solution.py:670
  46.7 0.9 %copy.10 = bf16[128,3,1024]{2,0,1:T(8,128)(2,1)} copy(bf16[128,3,1024]{2,0,1:T(8,128)(2,1)S(1)} %bitcast.2) | data formatting | bytes 1572864
  47.6 0.6 %copy.11 = f32[3,7,1024]{2,1,0:T(8,128)} copy(f32[3,7,1024]{2,1,0:T(8,128)S(1)} %get-tuple-element.13) | data formatting | bytes 172032
  48.3 0.6 %copy.12 = f32[8,32]{1,0:T(8,128)} copy(f32[8,32]{1,0:T(8,128)S(1)} %get-tuple-element.14) | data formatting | bytes 2048

commit v6 on v5

--- a/solution.py
+++ b/solution.py
@@ -234,11 +234,15 @@
     return both[:, :width] + both[:, width:] + dot32(lo, signal[:, :width])
 
 
+EARLY = (slice(0, 1), slice(1, 3))
+LATE = (slice(1, 3), slice(0, 1))
+
+
 def resident_kernel(
     ns, nc, kt, groups,
     proj, cot, weight_in, filt_in,
     gp_out, gs_out, gf_out,
-    weight, filt, packed, pin, halo, wide, feat, mixed, gated, part, part_edge, fgrad, gp_send,
+    weight, filt, packed, pin, halo, wide, feat, mixed, gated, part, fgrad, gp_send,
     tap_send, taps, low_hi, low_lo, up_hi, up_lo, gram,
     fa_send, fa_recv, fb_send, fb_recv, gs_acc, gs_send, gs_pair, gs_sum, gs_recv,
     local_sem, pack_sem, tap_ssem, tap_rsem, in_send, in_recv, gp_ssem, gp_rsem, gs_ssem, gs_rsem,
@@ -301,7 +305,7 @@
 
     def halo_copy(q, t, src, first):
         return send_to(
-            packed.at[lax.rem(q, hs) * 2 + t, 0:3, pl.ds(first, 16)], halo.at[t],
+            packed.at[lax.rem(q, hs) * 2 + t, :, pl.ds(first, 16)], halo.at[t],
             in_send.at[t, 1, q], in_recv.at[t, 1, 0], (q, mych),
         )
 
@@ -472,6 +476,34 @@
     near_pairs = [(b, c) for b in range(per) for c in range(b, per)]
     far_pairs = [(b, c) for b in range(per) for c in range(per, 2 * per)]
 
+    def finish_block(streams, t, i, carry):
+        b = lax.rem(mine + 1 + i, hs)
+        base = pl.multiple_of(b * LANES, LANES)
+        for p in range(LANES // ROWS):
+            first = base + p * ROWS
+            for j in range(streams.start, streams.stop):
+                acc = jnp.zeros((ROWS, LANES), jnp.float32)
+                source = wide[j, pl.ds(own_base + first + 8, ROWS), :]
+                for k in range(kt):
+                    shifted = fgrad[j, pl.ds(first + k, ROWS), :]
+                    acc = acc + weight[t, j, k : k + 1, :] * shifted
+                    terms = (shifted * source).reshape(ROWS // 8, 8, LANES)
+                    gs_acc[t, j, k] += jnp.sum(terms, 0)
+                gp_send[t, j, pl.ds(first, ROWS), :] = acc.astype(jnp.bfloat16)
+
+        @pl.when(i < hs - 1)
+        def _():
+            gp_copy(half * hs + b, t, me, streams).start()
+
+        return carry
+
+    def gp_copy(q, t, src, streams):
+        return send_to(
+            gp_send.at[t, streams, tile(lax.rem(q, hs)), :],
+            gp_out.at[streams, :, lanes_of(src, t)],
+            gp_ssem.at[t, streams.start % 2, q], gp_rsem.at[t, streams.start % 2, src], (q, mych),
+        )
+
     def early_part(t):
         for j in (1, 2):
             wide[j, 8 + span : 8 + span + 16, :] = halo[t, place[j]].astype(jnp.float32)
@@ -484,12 +516,15 @@
         for b in range(per):
             grads_of(t, local_rows[b], conv=conv_of(b, 0, (b + 1) * WIDE))
             part[local_rows[b], :] = corr_of(b, b * WIDE, span)
-        part_edge[...] = conv_of(per, 0, span + LANES, 16)
+        edge_conv = conv_of(per, 0, span + LANES, 16)
+        fgrad[0, edge, :] = halo[t, 3].astype(jnp.float32) * edge_conv
+        lax.fori_loop(0, hs, functools.partial(finish_block, EARLY[0], t), 0)
         add_gram(near_pairs)
         lax.fori_loop(0, hs, functools.partial(far_block, True, t), 0)
         for b in range(per):
             grads_of(t, local_rows[b], corr=part[local_rows[b], :] + corr_of(b, span, total))
-        grads_of(t, edge, conv=part_edge[...], corr=corr_of(per, span, total, 16))
+        grads_of(t, edge, corr=corr_of(per, span, total, 16))
+        lax.fori_loop(0, hs - 1, functools.partial(finish_block, EARLY[1], t), 0)
 
     def late_part(t):
         for j in range(3):
@@ -498,37 +533,12 @@
         for b in range(per):
             grads_of(t, local_rows[b], corr=corr_of(per + b, span + b * WIDE, total))
             part[local_rows[b], :] = conv_of(per + b, span, span + (b + 1) * WIDE)
+        lax.fori_loop(0, hs, functools.partial(finish_block, LATE[0], t), 0)
         add_gram([(per + b, per + c) for b, c in near_pairs])
         lax.fori_loop(0, hs, functools.partial(far_block, False, t), 0)
         for b in range(per):
             grads_of(t, local_rows[b], conv=part[local_rows[b], :] + conv_of(per + b, 0, span))
-
-    def finish_block(t, i, carry):
-        b = lax.rem(mine + 1 + i, hs)
-        base = pl.multiple_of(b * LANES, LANES)
-        for p in range(LANES // ROWS):
-            first = base + p * ROWS
-            for j in range(3):
-                acc = jnp.zeros((ROWS, LANES), jnp.float32)
-                source = wide[j, pl.ds(own_base + first + 8, ROWS), :]
-                for k in range(kt):
-                    shifted = fgrad[j, pl.ds(first + k, ROWS), :]
-                    acc = acc + weight[t, j, k : k + 1, :] * shifted
-                    terms = (shifted * source).reshape(ROWS // 8, 8, LANES)
-                    gs_acc[t, j, k] += jnp.sum(terms, 0)
-                gp_send[t, j, pl.ds(first, ROWS), :] = acc.astype(jnp.bfloat16)
-
-        @pl.when(i < hs - 1)
-        def _():
-            gp_copy(half * hs + b, t, me).start()
-
-        return carry
-
-    def gp_copy(q, t, src):
-        return send_to(
-            gp_send.at[t, :, tile(lax.rem(q, hs)), :], gp_out.at[:, :, lanes_of(src, t)],
-            gp_ssem.at[t, q], gp_rsem.at[t, src], (q, mych),
-        )
+        lax.fori_loop(0, hs - 1, functools.partial(finish_block, LATE[1], t), 0)
 
     filter_scale = 1.0 / math.sqrt(total * group_owners * WIDE)
     fa_copy = lambda q, src: send_to(
@@ -543,8 +553,6 @@
         @pl.when(half == 1)
         def _():
             late_part(t)
-
-        lax.fori_loop(0, hs - 1, functools.partial(finish_block, t), 0)
 
         @pl.when(t == half)
         def _():
@@ -558,7 +566,14 @@
                 fa_copy(q, me).start()
             fa_recv[me] = fa_send[me]
 
-        finish_block(t, hs - 1, carry)
+        @pl.when(half == 0)
+        def _():
+            finish_block(EARLY[1], t, hs - 1, carry)
+
+        @pl.when(half == 1)
+        def _():
+            finish_block(LATE[1], t, hs - 1, carry)
+
         gp_out[:, :, lanes_of(me, t)] = gp_send[t, :, tile(mine), :]
         return carry
 
@@ -627,19 +642,26 @@
         for t in range(2):
             for copy in near_copies(q, t, me):
                 copy.wait_send()
-            gp_copy(q, t, me).wait_send()
-            gp_copy(q, t, q).wait_recv()
     for _, c in ch_peers:
         fb_copy(c, mych).wait_send()
 
+    def returned(parts):
+        for q in near:
+            for t in range(2):
+                for streams in parts:
+                    gp_copy(q, t, me, streams).wait_send()
+                    gp_copy(q, t, q, streams).wait_recv()
+
     @pl.when(half == 0)
     def _():
+        returned(EARLY)
         for q in far:
             for t in range(2):
                 mix_copy(q, t, me).wait_send()
 
     @pl.when(half == 1)
     def _():
+        returned(LATE)
         for q in far:
             for t in range(2):
                 for copy in gate_copies(q, t, me):
@@ -681,13 +703,12 @@
             pltpu.VMEM((groups, LANES), f32),
             pltpu.VMEM((ns, 4, LANES, LANES), bf16),
             pltpu.VMEM((2, ns, 4, LANES, LANES), bf16),
-            pltpu.VMEM((2, 3, 16, LANES), bf16),
+            pltpu.VMEM((2, 4, 16, LANES), bf16),
             pltpu.VMEM((3, total + 8, LANES), f32),
             pltpu.VMEM((2, span + 16, LANES), f32),
             pltpu.VMEM((total, WIDE), bf16),
             pltpu.VMEM((total, WIDE), bf16),
             pltpu.VMEM((span, LANES), f32),
-            pltpu.VMEM((16, LANES), f32),
             pltpu.VMEM((3, span + 16, LANES), f32),
             pltpu.VMEM((2, 3, span, LANES), bf16),
             pltpu.VMEM((groups, 8, LANES), f32),
@@ -709,7 +730,7 @@
             dma((3,)), dma((3, ns)),
             dma((ns,)), dma((ns,)),
             dma((2, 2, ns)), dma((2, 2, ns)),
-            dma((2, ns)), dma((2, ns)),
+            dma((2, 2, ns)), dma((2, 2, ns)),
             dma((ns,)), dma((ns,)),
             dma((ns,)), dma((ns,)),
             dma((nc,)), dma((nc,)),

time: 49 us -> 49.3 us (level)
  no operation moved by 1% of the time
where the time goes in v6:
time: 49.3 us; the launch traced here: 49.2 us
  Pallas kernels  46.4 us (94%)
  local copies, waits for them, and re-layouts  2.11 us (4%)
  between operations  0.64 us (1%)
    pallas_call x1, Pallas kernels, resident(): pl.pallas_call(functools.partial(resident_kernel, ns, nc, kt, groups), ou...  46.4 us
    unnamed x3, local copies, waits for them, and re-layouts  2.11 us

profile of v6, /device:TPU:0, one launch (start us, length us, event | category | flops | bytes accessed | tf_op | source)
XLA Modules:
  0.0 49.2 jit_solution(1604946450458060177)
XLA Ops:
  0.6 46.4 %shard_map.67 = (bf16[3,128,1024]{2,1,0:T(8,128)(2,1)S(1)}, f32[3,7,1024]{2,1,0:T(8,128)S(1)}, f32[8,32]{1,0:T(8,128)S(1)}) custom-call(bf16[3,128,1024]{2,1,0:T(8,128)(2,1)} %bitcast.3, bf16[128,1024]{1,0:T(8,128)(2,1)} %cot.1, f32[3,7,1024]{2,1,0:T(8,128)} %weight_in.1, f32[2,128]{1,0:T(2,128)} %filt_in.1), custom_call_target="tpu_custom_call" | custom-call | tf_op jit(solution)/shard_map/pallas_call | solution.py:692
  47.1 0.9 %copy.10 = bf16[128,3,1024]{2,0,1:T(8,128)(2,1)} copy(bf16[128,3,1024]{2,0,1:T(8,128)(2,1)S(1)} %bitcast.2) | data formatting | bytes 1572864
  47.9 0.6 %copy.11 = f32[3,7,1024]{2,1,0:T(8,128)} copy(f32[3,7,1024]{2,1,0:T(8,128)S(1)} %get-tuple-element.13) | data formatting | bytes 172032
  48.6 0.6 %copy.12 = f32[8,32]{1,0:T(8,128)} copy(f32[8,32]{1,0:T(8,128)S(1)} %get-tuple-element.14) | data formatting | bytes 2048

commit v7 on v5

--- a/solution.py
+++ b/solution.py
@@ -12,7 +12,7 @@
 MESH = pl.DeviceIdType.MESH
 LANES = 128
 WIDE = 256
-ROWS = 64
+ROWS = 128
 
 
 def passed_along(block, axis, distance):

time: 49 us -> 49 us (level)
  no operation moved by 1% of the time
where the time goes in v7:
time: 49 us; the launch traced here: 48.9 us
  Pallas kernels  46.1 us (94%)
  local copies, waits for them, and re-layouts  2.11 us (4%)
  between operations  0.64 us (1%)
    pallas_call x1, Pallas kernels, resident(): pl.pallas_call(functools.partial(resident_kernel, ns, nc, kt, groups), ou...  46.1 us
    unnamed x3, local copies, waits for them, and re-layouts  2.11 us

profile of v7, /device:TPU:0, one launch (start us, length us, event | category | flops | bytes accessed | tf_op | source)
XLA Modules:
  0.0 48.9 jit_solution(10068663771132154035)
XLA Ops:
  0.6 46.1 %shard_map.67 = (bf16[3,128,1024]{2,1,0:T(8,128)(2,1)S(1)}, f32[3,7,1024]{2,1,0:T(8,128)S(1)}, f32[8,32]{1,0:T(8,128)S(1)}) custom-call(bf16[3,128,1024]{2,1,0:T(8,128)(2,1)} %bitcast.3, bf16[128,1024]{1,0:T(8,128)(2,1)} %cot.1, f32[3,7,1024]{2,1,0:T(8,128)} %weight_in.1, f32[2,128]{1,0:T(2,128)} %filt_in.1), custom_call_target="tpu_custom_call" | custom-call | tf_op jit(solution)/shard_map/pallas_call | solution.py:670
  46.7 0.9 %copy.10 = bf16[128,3,1024]{2,0,1:T(8,128)(2,1)} copy(bf16[128,3,1024]{2,0,1:T(8,128)(2,1)S(1)} %bitcast.2) | data formatting | bytes 1572864
  47.6 0.6 %copy.11 = f32[3,7,1024]{2,1,0:T(8,128)} copy(f32[3,7,1024]{2,1,0:T(8,128)S(1)} %get-tuple-element.13) | data formatting | bytes 172032
  48.3 0.6 %copy.12 = f32[8,32]{1,0:T(8,128)} copy(f32[8,32]{1,0:T(8,128)S(1)} %get-tuple-element.14) | data formatting | bytes 2048
